TPU v7x, 128 devices: a whole 4x4x4 slice. The times are simulated.
128 devices in a mesh: kv: 32 (over z, x, core), tp: 4 (over y).
Axes of the slice: x: 4, y: 4, z: 4, core: 2. Of those that a mesh axis runs over, the one named last changes fastest.
Arguments:
- query: bfloat16 [4, 128, 128], P(None, 'tp'), may hold values from -8 to 28
- key_cache: bfloat16 [8192, 16, 8, 128], P('kv', None, 'tp'), may hold values from -6 to 7
- value_cache: bfloat16 [8192, 16, 8, 128], P('kv', None, 'tp'), may hold values from -6 to 6
- seq_lengths: int32 [4], replicated, may hold values from 1 to 32768, as said below
- block_table: int32 [4, 2048], P(None, 'kv'), may hold values from 0 to 255, as said below
- residual: bfloat16 [4, 16384], replicated, may hold values from -6 to 6
- norm_gain: bfloat16 [16384], replicated, may hold values from 0.099609375 to 1.8984375
- gate_weight: bfloat16 [26624, 16384], P(('kv', 'tp')), may hold values from -0.046875 to 0.046875
- up_weight: bfloat16 [26624, 16384], P(('kv', 'tp')), may hold values from -0.046875 to 0.046875
- down_weight: bfloat16 [26624, 16384], P(('kv', 'tp')), may hold values from -0.125 to 0.125
Outputs:
- layer_out: bfloat16 [4, 16384], P(None, ('kv', 'tp'))
- attention: bfloat16 [4, 128, 128], P(None, 'tp')
Inputs may be any that keep to these rules, and one draw needn't show every extreme that they name: `seq_lengths`: each sequence has at least one live position; some sequence has all 32768 positions live. `block_table`: for each index of kv, the columns of its 64 logical blocks hold, over all rows together, every page number once.
All inputs are finite; a program needn't handle non-finite values.
Results may differ from a plain program's by a relative error of at most 0.01.
Values may be sent and summed in bfloat16 or wider, within the bound.
No kernel may reach another device: no remote copies, remote signals or barrier semaphores. Data moves between devices by JAX's collectives and lax.ppermute only.
A program may use at most 128 MiB of HBM per device.

v0:
```python
import jax
import jax.numpy as jnp
from jax import lax
from jax.sharding import PartitionSpec as P

NEG = -1e30


def local_partials(query, key_cache, value_cache, seq_lengths, block_table):
    row_count, head_count, head_width = query.shape
    local_heads = key_cache.shape[2]
    group_size = head_count // local_heads
    page_size = key_cache.shape[1]
    span_cells = block_table.shape[1] * page_size
    keys_row = key_cache[block_table].reshape(row_count, span_cells, local_heads, head_width)
    values_row = value_cache[block_table].reshape(row_count, span_cells, local_heads, head_width)
    first_cell = lax.axis_index("kv") * span_cells
    position = first_cell + jnp.arange(span_cells, dtype=jnp.int32)
    active = (position[None, :] < seq_lengths[:, None])[:, None, None, :]
    grouped = query.reshape(row_count, local_heads, group_size, head_width)
    scores = jnp.einsum(
        "bgqd,bcgd->bgqc", grouped, keys_row, preferred_element_type=jnp.float32
    ) * head_width ** (-0.5)
    masked = jnp.where(active, scores, NEG)
    top_score = jnp.max(masked, axis=-1)
    weights = jnp.where(active, jnp.exp(masked - top_score[..., None]), 0.0)
    denominator = jnp.sum(weights, axis=-1)
    summed = jnp.einsum(
        "bgqc,bcgd->bgqd",
        weights.astype(jnp.bfloat16),
        values_row,
        preferred_element_type=jnp.float32,
    )
    return (
        top_score.reshape(row_count, head_count),
        denominator.reshape(row_count, head_count),
        summed.reshape(row_count, head_count, head_width),
    )


def merge_blocks(top_all, denom_all, summed_all):
    highest = jnp.max(top_all, axis=0)
    factor = jnp.exp(top_all - highest[None])
    denominator = jnp.sum(factor * denom_all, axis=0)
    summed = jnp.sum(factor[..., None] * summed_all, axis=0)
    return (summed / denominator[..., None]).astype(jnp.bfloat16)


def shards(
    query,
    key_cache,
    value_cache,
    seq_lengths,
    block_table,
    residual,
    norm_gain,
    gate_weight,
    up_weight,
    down_weight,
):
    top_score, denominator, summed = local_partials(
        query, key_cache, value_cache, seq_lengths, block_table
    )
    finished = merge_blocks(
        lax.all_to_all(top_score[None], "kv", split_axis=2, concat_axis=0, tiled=True),
        lax.all_to_all(denominator[None], "kv", split_axis=2, concat_axis=0, tiled=True),
        lax.all_to_all(summed[None], "kv", split_axis=2, concat_axis=0, tiled=True),
    )
    attention = lax.all_gather(finished, "kv", axis=1, tiled=True)
    full_heads = lax.all_gather(attention, "tp", axis=1, tiled=True)
    row_count = residual.shape[0]
    hidden_state = residual.astype(jnp.float32) + full_heads.reshape(row_count, -1).astype(
        jnp.float32
    )
    mean_square = jnp.mean(hidden_state * hidden_state, axis=-1, keepdims=True)
    normed = (hidden_state * lax.rsqrt(mean_square + 1e-05) * norm_gain.astype(jnp.float32)).astype(
        jnp.bfloat16
    )
    gate_value = jnp.einsum("bd,fd->bf", normed, gate_weight, preferred_element_type=jnp.float32)
    up_value = jnp.einsum("bd,fd->bf", normed, up_weight, preferred_element_type=jnp.float32)
    activated = (jax.nn.silu(gate_value) * up_value).astype(jnp.bfloat16)
    mixed = jnp.dot(activated, down_weight, preferred_element_type=jnp.float32)
    share_width = hidden_state.shape[1] // lax.axis_size(("kv", "tp"))
    share_start = lax.axis_index(("kv", "tp")) * share_width
    totals = lax.psum(mixed, ("kv", "tp"))
    layer_out = lax.dynamic_slice_in_dim(hidden_state + totals, share_start, share_width, 1)
    return (layer_out.astype(jnp.bfloat16), attention)


def solution(mesh):
    placed = (
        P(None, "tp", None),
        P("kv", None, "tp", None),
        P("kv", None, "tp", None),
        P(),
        P(None, "kv"),
        P(),
        P(),
        P(("kv", "tp"), None),
        P(("kv", "tp"), None),
        P(("kv", "tp"), None),
    )
    return jax.shard_map(
        shards,
        mesh=mesh,
        in_specs=placed,
        out_specs=(P(None, ("kv", "tp")), P(None, "tp", None)),
        check_vma=False,
    )
```

profile of v0, /device:TPU:1, one launch (start us, length us, event | category | flops | bytes accessed | tf_op | source)
XLA Modules:
  0.0 271.9 jit_solution(15854602702053174173)
XLA Ops:
  7.2 0.8 compare_select_fusion
  8.0 0.1 reshape.175
  8.1 0.7 broadcast_compare_fusion
  8.9 10.5 %gather_fusion = bf16[256,16,2,128]{3,2,1,0:T(2,128)(2,1)} fusion(bf16[256,16,2,128]{3,2,1,0:T(2,128)(2,1)S(1)} %copy-done, s32[1024]{0:T(1024)S(1)} %pad_clamp_fusion), kind=kCustom, calls=%fused_computation | custom fusion | bytes 4195328 | tf_op jit(solution)/shard_map/gather | solution.py:15
  19.4 2.3 fusion.34
  21.7 0.7 copy.32
  22.5 9.4 %all-to-all-start = ((f32[1,4,32]{1,0,2:T(1,128)}), f32[1,4,32]{1,0,2:T(1,128)S(1)}, u32[]{:S(2)}, u32[]{:S(2)}) async-start(f32[1,4,32]{1,0,2:T(1,128)} %bitcast.3), calls=%async_computation | async-start | bytes 32768 | tf_op jit(solution)/shard_map/all_to_all | solution.py:65
  31.9 12.1 %gather_fusion.1 = bf16[256,16,2,128]{3,2,1,0:T(2,128)(2,1)} fusion(bf16[256,16,2,128]{3,2,1,0:T(2,128)(2,1)} %param.12, s32[1024]{0:T(1024)S(1)} %pad_clamp_fusion), kind=kCustom, calls=%fused_computation.1 | custom fusion | bytes 4195328 | tf_op jit(solution)/shard_map/gather | solution.py:16
  44.0 2.1 fusion
  46.1 0.2 fusion.15
  46.4 0.7 copy.28
  47.0 0.7 copy.33
  47.7 7.4 %all-to-all-start.2 = ((f32[1,4,32]{1,0,2:T(1,128)}), f32[1,4,32]{1,0,2:T(1,128)S(1)}, u32[]{:S(2)}, u32[]{:S(2)}) async-start(f32[1,4,32]{1,0,2:T(1,128)} %bitcast.15), calls=%async_computation.2 | async-start | bytes 32768 | tf_op jit(solution)/shard_map/all_to_all | solution.py:66
  55.1 0.1 copy.25
  55.2 0.1 reduce_max.19
  55.3 0.1 fusion.28
  55.3 0.1 copy.26
  55.4 6.6 %all-to-all-done.2 = f32[1,4,32]{1,0,2:T(1,128)S(1)} async-done(((f32[1,4,32]{1,0,2:T(1,128)}), f32[1,4,32]{1,0,2:T(1,128)S(1)}, u32[]{:S(2)}, u32[]{:S(2)}) %all-to-all-start.2) | async-done | bytes 544 | tf_op jit(solution)/shard_map/all_to_all | solution.py:66
  62.1 4.1 %all-to-all-start.1 = ((f32[1,4,32,128]{3,1,0,2:T(4,128)}), f32[1,4,32,128]{3,1,0,2:T(4,128)S(1)}, u32[]{:S(2)}, u32[]{:S(2)}) async-start(f32[1,4,32,128]{3,1,0,2:T(4,128)} %copy.28), calls=%async_computation.1 | async-start | bytes 131072 | tf_op jit(solution)/shard_map/all_to_all | solution.py:67
  66.3 0.1 copy.30
  66.4 0.2 fusion.26
  66.6 7.1 %all-to-all-done.1 = f32[1,4,32,128]{3,1,0,2:T(4,128)S(1)} async-done(((f32[1,4,32,128]{3,1,0,2:T(4,128)}), f32[1,4,32,128]{3,1,0,2:T(4,128)S(1)}, u32[]{:S(2)}, u32[]{:S(2)}) %all-to-all-start.1) | async-done | bytes 65568 | tf_op jit(solution)/shard_map/all_to_all | solution.py:67
  73.7 0.1 fusion.21
  73.8 0.1 fusion.30
  73.9 22.5 %all_gather.6 = bf16[4,32,128]{2,0,1:T(4,128)(2,1)S(1)} all-gather(bf16[4,1,128]{2,0,1:T(4,128)(2,1)S(1)} %fusion.30), channel_id=1, replica_groups=mesh['kv'=32,'tp'=4] {'kv'}, dimensions={1}, use_global_device_ids=true | all-gather | bytes 33792 | tf_op jit(solution)/shard_map/all_gather | solution.py:69
  96.4 10.2 %all_gather.7 = bf16[4,128,128]{2,0,1:T(4,128)(2,1)S(1)} all-gather(bf16[4,32,128]{2,0,1:T(4,128)(2,1)S(1)} %all_gather.6), channel_id=1, replica_groups=mesh['kv'=32,'tp'=4] {'tp'}, dimensions={1}, use_global_device_ids=true | all-gather | bytes 163840 | tf_op jit(solution)/shard_map/all_gather | solution.py:70
  106.6 0.2 convert_add_fusion
  106.9 4.8 %fusion.33 = f32[4,208]{1,0:T(4,128)S(1)} fusion(bf16[208,16384]{1,0:T(8,128)(2,1)} %param.17, f32[16384]{0:T(1024)S(1)} %convert_element_type.40, f32[4]{0:T(128)S(1)} %add_rsqrt_fusion, bf16[4,128,128]{2,0,1:T(4,128)(2,1)S(1)} %all_gather.7, bf16[4,16384]{1,0:T(4,128)(2,1)S(1)} %copy-done.1), kind=kOutput, calls=%fused_computation.45 | convolution fusion | flops 27656192 | bytes 7146768 | tf_op jit(solution)/shard_map/bd,fd->bf/dot_general | solution.py:79
  111.7 10.2 %fusion.14 = f32[4,16384]{1,0:T(4,128)} fusion(bf16[208,16384]{1,0:T(8,128)(2,1)} %param.19, bf16[208,16384]{1,0:T(8,128)(2,1)} %param.18, f32[4,208]{1,0:T(4,128)S(1)} %fusion.33, f32[16384]{0:T(1024)S(1)} %convert_element_type.40, f32[4]{0:T(128)S(1)} %add_rsqrt_fusion, bf16[4,128,128]{2,0,1:T(4,128)(2,1)S(1)} %all_gather.7, ...), kind=kOutput, calls=%fused_computation.11 | convolution fusion | flops 54924160 | bytes 14224656 | tf_op jit(solution)/shard_map/dot_general | solution.py:82
  121.9 0.6 copy.31
  122.5 141.3 %all-reduce.2.cloned.1.call-done = f32[4,16384]{1,0:T(4,128)} async-done(((f32[4,16384]{1,0:T(4,128)}), f32[4,16384]{1,0:T(4,128)}) %all-reduce.2.cloned.1.call-update) | async-done | bytes 262160 | tf_op jit(solution)/shard_map/psum | solution.py:85
  263.8 1.2 fusion.25
  (15 shorter events, 0.1 us)
Async XLA Ops:
  7.2 1.7 copy-start
  8.9 10.6 %copy-start.3 = (bf16[4,32,128]{2,1,0:T(8,128)(2,1)S(1)}, bf16[4,32,128]{2,1,0:T(8,128)(2,1)}, u32[]{:S(2)}) copy-start(bf16[4,32,128]{2,1,0:T(8,128)(2,1)} %param.10) | copy-start | bytes 98308
  22.5 25.3 %all-to-all-start = ((f32[1,4,32]{1,0,2:T(1,128)}), f32[1,4,32]{1,0,2:T(1,128)S(1)}, u32[]{:S(2)}, u32[]{:S(2)}) async-start(f32[1,4,32]{1,0,2:T(1,128)} %bitcast.3), calls=%async_computation | async-start | bytes 32768 | tf_op jit(solution)/shard_map/all_to_all | solution.py:65
  44.0 3.7 %copy-start.2 = (bf16[16384]{0:T(1024)(128)(2,1)S(1)}, bf16[16384]{0:T(1024)(128)(2,1)}, u32[]{:S(2)}) copy-start(bf16[16384]{0:T(1024)(128)(2,1)} %param.16) | copy-start | bytes 98308
  44.0 62.6 %copy-start.1 = (bf16[4,16384]{1,0:T(4,128)(2,1)S(1)}, bf16[4,16384]{1,0:T(4,128)(2,1)}, u32[]{:S(2)}) copy-start(bf16[4,16384]{1,0:T(4,128)(2,1)} %param.15) | copy-start | bytes 393220
  47.7 14.3 %all-to-all-start.2 = ((f32[1,4,32]{1,0,2:T(1,128)}), f32[1,4,32]{1,0,2:T(1,128)S(1)}, u32[]{:S(2)}, u32[]{:S(2)}) async-start(f32[1,4,32]{1,0,2:T(1,128)} %bitcast.15), calls=%async_computation.2 | async-start | bytes 32768 | tf_op jit(solution)/shard_map/all_to_all | solution.py:66
  62.1 11.6 %all-to-all-start.1 = ((f32[1,4,32,128]{3,1,0,2:T(4,128)}), f32[1,4,32,128]{3,1,0,2:T(4,128)S(1)}, u32[]{:S(2)}, u32[]{:S(2)}) async-start(f32[1,4,32,128]{3,1,0,2:T(4,128)} %copy.28), calls=%async_computation.1 | async-start | bytes 131072 | tf_op jit(solution)/shard_map/all_to_all | solution.py:67
  66.2 197.5 %all-reduce.2.cloned.1.call-start = ((), (), s32[]{:S(2)}) async-start(), calls=%async_computation.3 | async-start | bytes 524288 | tf_op jit(solution)/shard_map/psum | solution.py:85
Sparse Core Ops, SparseCore 0:
  122.0 141.7 all-reduce.1
where the time goes:
time: 272 us
  waiting for transfers between devices  155 us (57%)
  blocking collectives  32.7 us (12%)
  local copies, waits for them, and re-layouts  25.7 us (9%)
  starting transfers between devices  21 us (8%)
  matrix products  19.4 us (7%)
  between operations  14.1 us (5%)
  other arithmetic  3.81 us (1%)
    psum x1, waiting for transfers between devices, shards(): totals = lax.psum(mixed, ('kv', 'tp'))  141 us
    all_gather x1, blocking collectives, shards(): attention = lax.all_gather(finished, 'kv', axis=1, tiled=True)  22.5 us
    gather x1, local copies, waits for them, and re-layouts, local_partials(): value_cache[block_table]  12.1 us
    gather x1, local copies, waits for them, and re-layouts, local_partials(): key_cache[block_table]  10.5 us
    all_gather x1, blocking collectives, shards(): full_heads = lax.all_gather(attention, 'tp', axis=1, tiled=True)  10.2 us
    dot_general x1, matrix products, shards(): mixed = jnp.dot(activated, down_weight, preferred_element_type=jnp.float32)  10.2 us
    all_to_all x1, starting transfers between devices, shards(): lax.all_to_all(top_score[None], 'kv', split_axis=2, concat_axis=0, tiled=...  9.43 us
    all_to_all x1, starting transfers between devices, shards(): lax.all_to_all(denominator[None], 'kv', split_axis=2, concat_axis=0, tile...  7.39 us
  transfers between devices with their start and end apart: 4, of which 3 were waited for; matrix products, arithmetic and copies ran while one was open for 6% of the time, Pallas kernels for 0%

commit v1 on v0

v1 whole, which is shorter than its diff:
```python
import functools

import jax
import jax.numpy as jnp
from jax import lax
from jax.experimental import pallas as pl
from jax.experimental.pallas import tpu as pltpu
from jax.sharding import PartitionSpec as P

NEG = -1e30
F32 = jnp.float32
BF16 = jnp.bfloat16
MIB = 1 << 20
NT = (((1,), (1,)), ((), ()))
PAGES_PER_DOT = 8


def attention_kernel(lengths, table, query, keys, values, out, k_vmem, v_vmem, sems):
    rows, heads, width = query.shape
    pages = table.shape[1]
    cells = keys.shape[0] // (rows * pages)
    k_copy = pltpu.make_async_copy(keys, k_vmem, sems.at[0])
    v_copy = pltpu.make_async_copy(values, v_vmem, sems.at[1])
    k_copy.start()
    v_copy.start()
    first = lax.axis_index("kv") * (pages * cells // 2)
    span = pages * cells
    column = lax.broadcasted_iota(jnp.int32, (heads, span), 1)
    head = lax.broadcasted_iota(jnp.int32, (heads, span), 0)
    own = (column % 2) == (head // (heads // 2))
    position = jnp.where(own, first + column // 2, jnp.int32(2**30))
    lane = lax.broadcasted_iota(jnp.int32, (heads, width), 1)

    def block(ref, row, at):
        return jnp.concatenate(
            [
                ref[pl.ds(pl.multiple_of(table[row, at + i] * cells, cells), cells), :]
                for i in range(PAGES_PER_DOT)
            ],
            axis=0,
        )

    kept = []
    k_copy.wait()
    for row in range(rows):
        q = query[row]
        scores = jnp.concatenate(
            [
                lax.dot_general(q, block(k_vmem, row, at), NT, preferred_element_type=F32)
                for at in range(0, pages, PAGES_PER_DOT)
            ],
            axis=1,
        ) * (width**-0.5)
        active = position < lengths[row]
        masked = jnp.where(active, scores, NEG)
        top = jnp.max(masked, axis=-1, keepdims=True)
        weights = jnp.where(active, jnp.exp(masked - top), 0.0)
        total = jnp.sum(weights, axis=-1, keepdims=True)
        kept.append(weights.astype(BF16))
        out[:, rows + row, :] = jnp.where(lane < width // 2, top, total)
    v_copy.wait()
    for row in range(rows):
        summed = jnp.zeros((heads, width), F32)
        for at in range(0, pages, PAGES_PER_DOT):
            summed += jnp.dot(
                kept[row][:, at * cells : (at + PAGES_PER_DOT) * cells],
                block(v_vmem, row, at),
                preferred_element_type=F32,
            )
        out[:, row, :] = summed


def merge_kernel(parts, out):
    count, double, width = parts.shape
    rows = double // 2
    stats = parts[:, rows:, :]
    top = stats[:, :, 0:1]
    total = stats[:, :, width // 2 : width // 2 + 1]
    highest = jnp.max(top, axis=0, keepdims=True)
    factor = jnp.exp(top - highest)
    denominator = jnp.sum(factor * total, axis=0)
    summed = jnp.sum(factor * parts[:, :rows, :], axis=0)
    done = (summed / denominator).astype(BF16)
    out[...] = jnp.broadcast_to(done[None], out.shape)


def feed_kernel(heads, residual, gain, gate_w, up_w, down_w, out, normed, chunk):
    count, rows, width = heads.shape
    features = count * width
    squares = jnp.zeros((rows, width), F32)
    for i in range(count):
        cols = slice(i * width, (i + 1) * width)
        hidden = residual[:, cols].astype(F32) + heads[i].astype(F32)
        squares += hidden * hidden
    mean_square = jnp.sum(squares, axis=-1, keepdims=True) / features
    scale = lax.rsqrt(mean_square + 1e-05)
    for i in range(count):
        cols = slice(i * width, (i + 1) * width)
        hidden = residual[:, cols].astype(F32) + heads[i].astype(F32)
        normed[:, cols] = (hidden * scale * gain[:, cols].astype(F32)).astype(BF16)
    units = gate_w.shape[0]
    gate = jnp.zeros((rows, units), F32)
    up = jnp.zeros((rows, units), F32)
    for at in range(0, features, chunk):
        x = normed[:, at : at + chunk]
        gate += lax.dot_general(x, gate_w[:, at : at + chunk], NT, preferred_element_type=F32)
        up += lax.dot_general(x, up_w[:, at : at + chunk], NT, preferred_element_type=F32)
    activated = (gate / (1.0 + jnp.exp(-gate)) * up).astype(BF16)
    for at in range(0, features, chunk):
        mixed = jnp.dot(activated, down_w[:, at : at + chunk], preferred_element_type=F32)
        for j in range(chunk // width):
            out[at // width + j] = mixed[:, j * width : (j + 1) * width]


def final_kernel(parts, heads, residual, out):
    count, rows, width = parts.shape
    share = lax.axis_index("kv") * lax.axis_size("tp") + lax.axis_index("tp")
    cols = pl.ds(pl.multiple_of(share * width, width), width)
    hidden = residual[:, cols].astype(F32) + heads[share].astype(F32)
    out[...] = (hidden + jnp.sum(parts[...], axis=0)).astype(BF16)


VMEM = pl.BlockSpec(memory_space=pltpu.VMEM)
SMEM = pl.BlockSpec(memory_space=pltpu.SMEM)
ANY = pl.BlockSpec(memory_space=pl.ANY)


def in_vmem(x):
    return pltpu.with_memory_space_constraint(x, pltpu.VMEM)


def shards(
    query,
    key_cache,
    value_cache,
    seq_lengths,
    block_table,
    residual,
    norm_gain,
    gate_weight,
    up_weight,
    down_weight,
):
    rows, heads, width = query.shape
    keys = key_cache.reshape(-1, width)
    values = value_cache.reshape(-1, width)
    kv_size, tp_size = lax.axis_size("kv"), lax.axis_size("tp")
    devices = kv_size * tp_size
    partials = pl.pallas_call(
        attention_kernel,
        out_shape=jax.ShapeDtypeStruct((heads, 2 * rows, width), F32),
        in_specs=[SMEM, SMEM, VMEM, ANY, ANY],
        out_specs=VMEM,
        scratch_shapes=[
            pltpu.VMEM(keys.shape, BF16),
            pltpu.VMEM(values.shape, BF16),
            pltpu.SemaphoreType.DMA((2,)),
        ],
        compiler_params=pltpu.CompilerParams(vmem_limit_bytes=16 * MIB),
        name="attention_partials",
    )(seq_lengths, block_table, query, keys, values)
    gathered = lax.all_to_all(partials, "kv", 0, 0, tiled=True)
    finished = pl.pallas_call(
        merge_kernel,
        out_shape=jax.ShapeDtypeStruct((devices, rows, width), BF16),
        in_specs=[VMEM],
        out_specs=VMEM,
        compiler_params=pltpu.CompilerParams(vmem_limit_bytes=16 * MIB),
        name="merge_blocks",
    )(gathered)
    all_heads = lax.all_to_all(finished, ("tp", "kv"), 0, 0, tiled=True)
    mixed = pl.pallas_call(
        functools.partial(feed_kernel, chunk=2048),
        out_shape=jax.ShapeDtypeStruct((devices, rows, width), F32),
        in_specs=[VMEM] * 6,
        out_specs=VMEM,
        scratch_shapes=[pltpu.VMEM((rows, devices * width), BF16)],
        compiler_params=pltpu.CompilerParams(vmem_limit_bytes=16 * MIB),
        name="feed_forward",
    )(
        all_heads,
        residual,
        norm_gain.reshape(1, -1),
        in_vmem(gate_weight),
        in_vmem(up_weight),
        in_vmem(down_weight),
    )
    sums = lax.all_to_all(mixed, ("kv", "tp"), 0, 0, tiled=True)
    layer_out = pl.pallas_call(
        final_kernel,
        out_shape=jax.ShapeDtypeStruct((rows, width), BF16),
        in_specs=[VMEM] * 3,
        out_specs=VMEM,
        compiler_params=pltpu.CompilerParams(vmem_limit_bytes=16 * MIB),
        name="add_shares",
    )(sums, all_heads, residual)
    own_heads = lax.dynamic_slice_in_dim(all_heads, lax.axis_index("tp") * heads, heads, 0)
    return layer_out, own_heads.transpose(1, 0, 2)


def solution(mesh):
    placed = (
        P(None, "tp", None),
        P("kv", None, "tp", None),
        P("kv", None, "tp", None),
        P(),
        P(None, "kv"),
        P(),
        P(),
        P(("kv", "tp"), None),
        P(("kv", "tp"), None),
        P(("kv", "tp"), None),
    )
    return jax.shard_map(
        shards,
        mesh=mesh,
        in_specs=placed,
        out_specs=(P(None, ("kv", "tp")), P(None, "tp", None)),
        check_vma=False,
    )
```

time: 272 us -> 74 us (0.27)
  waiting for transfers between devices: 155 us -> 19.6 us
  matrix products: 19.4 us -> 0 us
  blocking collectives: 32.7 us -> 16.9 us
  between operations: 14.1 us -> 0.69 us
  starting transfers between devices: 21 us -> 10.2 us
  Pallas kernels: 0 us -> 9.66 us
  local copies, waits for them, and re-layouts: 25.7 us -> 16.4 us
  other arithmetic: 3.81 us -> 0 us
    psum x1 -> x0, waiting for transfers between devices: 141 us -> none  [shards(): totals = lax.psum(mixed, ('kv', 'tp'))]
    all_gather x2 -> x0, blocking collectives: 32.7 us -> none  [the longest x1 22.5 us: shards(): attention = lax.all_gather(finished, 'kv', axis=1, tiled=True)]
    gather x2 -> x0, local copies, waits for them, and re-layouts: 22.7 us -> none  [the longest x1 12.1 us: local_partials(): value_cache[block_table]]
    dot_general x4 -> x0, matrix products: 19.4 us -> none  [the longest x1 10.2 us: shards(): mixed = jnp.dot(activated, down_weight, preferred_element_type=jnp.float32)]
    all_to_all x0 -> x1, blocking collectives: none -> 16.9 us  [shards(): gathered = lax.all_to_all(partials, 'kv', 0, 0, tiled=True)]
    unnamed x9 -> x21, local copies, waits for them, and re-layouts: 0.64 us -> 15.6 us
    all_to_all x3 -> x2, starting transfers between devices: 21 us -> 10.2 us  [the longest x1 5.92 us: shards(): all_heads = lax.all_to_all(finished, ('tp', 'kv'), 0, 0, tiled=True)]
    pallas_call x0 -> x4, Pallas kernels: none -> 9.66 us  [the longest x1 5.49 us: shards(): pl.pallas_call(functools.partial(feed_kernel, chunk=2048), out_shape=jax....]
  transfers between devices with their start and end apart: 4 -> 2, of which waited for: 3 -> 2; matrix products, arithmetic and copies ran while one was open for 6% -> 2% of each run, Pallas kernels for 0% -> 0%
where the time goes in v1:
time: 74 us; the launch traced here: 73.4 us
  waiting for transfers between devices  19.6 us (26%)
  blocking collectives  16.9 us (23%)
  local copies, waits for them, and re-layouts  16.4 us (22%)
  starting transfers between devices  10.2 us (14%)
  Pallas kernels  9.66 us (13%)
    all_to_all x1, blocking collectives, shards(): gathered = lax.all_to_all(partials, 'kv', 0, 0, tiled=True)  16.9 us
    unnamed x21, local copies, waits for them, and re-layouts  15.6 us
    all_to_all x1, waiting for transfers between devices, shards(): sums = lax.all_to_all(mixed, ('kv', 'tp'), 0, 0, tiled=True)  10.5 us
    all_to_all x1, waiting for transfers between devices, shards(): all_heads = lax.all_to_all(finished, ('tp', 'kv'), 0, 0, tiled=True)  9.16 us
    all_to_all x1, starting transfers between devices, shards(): all_heads = lax.all_to_all(finished, ('tp', 'kv'), 0, 0, tiled=True)  5.92 us
    pallas_call x1, Pallas kernels, shards(): pl.pallas_call(functools.partial(feed_kernel, chunk=2048), out_shape=jax....  5.49 us
    all_to_all x1, starting transfers between devices, shards(): sums = lax.all_to_all(mixed, ('kv', 'tp'), 0, 0, tiled=True)  4.27 us
    pallas_call x1, Pallas kernels, shards(): pl.pallas_call(attention_kernel, out_shape=jax.ShapeDtypeStruct((heads, 2...  2.61 us
  transfers between devices with their start and end apart: 2, of which 2 were waited for; matrix products, arithmetic and copies ran while one was open for 2% of the time, Pallas kernels for 0%

profile of v1, /device:TPU:1, one launch (start us, length us, event | category | flops | bytes accessed | tf_op | source)
XLA Modules:
  0.0 73.4 jit_solution(2132322054394132056)
XLA Ops:
  0.6 0.0 copy-start.3
  0.6 1.6 %copy-done.3 = bf16[256,16,2,128]{3,2,1,0:T(2,128)(2,1)S(1)} copy-done((bf16[256,16,2,128]{3,2,1,0:T(2,128)(2,1)S(1)}, bf16[256,16,2,128]{3,2,1,0:T(2,128)(2,1)}, u32[]{:S(2)}) %copy-start.3) | copy-done | bytes 2097176
  2.2 0.0 copy-start.4
  2.2 1.6 %copy-done.4 = bf16[256,16,2,128]{3,2,1,0:T(2,128)(2,1)S(1)} copy-done((bf16[256,16,2,128]{3,2,1,0:T(2,128)(2,1)S(1)}, bf16[256,16,2,128]{3,2,1,0:T(2,128)(2,1)}, u32[]{:S(2)}) %copy-start.4) | copy-done | bytes 2097176
  3.8 0.0 copy-start.7
  3.8 0.8 %copy-done.7 = bf16[4,32,128]{2,1,0:T(8,128)(2,1)S(1)} copy-done((bf16[4,32,128]{2,1,0:T(8,128)(2,1)S(1)}, bf16[4,32,128]{2,1,0:T(8,128)(2,1)}, u32[]{:S(2)}) %copy-start.7) | copy-done | bytes 32792
  4.6 0.0 copy-start.8
  4.6 0.7 copy-done.8
  5.3 0.0 copy-start.9
  5.3 0.7 copy-done.9
  5.9 2.6 %attention_partials.1 = f32[32,8,128]{2,1,0:T(8,128)S(1)} custom-call(s32[4]{0:T(128)S(1)} %copy-done.9, s32[4,64]{1,0:T(4,128)S(1)} %copy-done.8, bf16[4,32,128]{2,1,0:T(8,128)(2,1)S(1)} %copy-done.7, bf16[8192,128]{1,0:T(8,128)(2,1)S(1)} %bitcast.4, bf16[8192,128]{1,0:T(8,128)(2,1)S(1)} %bitcast.5), custom_call_target="tpu_custom_call" | custom-call | tf_op jit(solution)/shard_map/attention_partials/pallas_call | solution.py:149
  8.5 16.9 %all_to_all.15.parts = f32[32,8,128]{2,1,0:T(8,128)S(1)} all-to-all(f32[32,8,128]{2,1,0:T(8,128)S(1)} %attention_partials.1), channel_id=1, replica_groups=mesh['kv'=32,'tp'=4] {'kv'}, dimensions={0} | all-to-all | bytes 262144 | tf_op jit(solution)/shard_map/all_to_all | solution.py:162
  25.4 0.9 %merge_blocks.1 = bf16[128,4,128]{2,1,0:T(4,128)(2,1)} custom-call(f32[32,8,128]{2,1,0:T(8,128)S(1)} %all_to_all.15.parts), custom_call_target="tpu_custom_call" | custom-call | tf_op jit(solution)/shard_map/merge_blocks/pallas_call | solution.py:163
  26.2 5.9 %all-to-all-start.1 = ((bf16[128,4,128]{2,1,0:T(4,128)(2,1)}), bf16[128,4,128]{2,1,0:T(4,128)(2,1)S(1)}, u32[]{:S(2)}, u32[]{:S(2)}) async-start(bf16[128,4,128]{2,1,0:T(4,128)(2,1)} %merge_blocks.1), calls=%async_computation.1 | async-start | bytes 262144 | tf_op jit(solution)/shard_map/all_to_all | solution.py:171
  32.2 0.8 %reshape.15.gain = bf16[1,16384]{1,0:T(2,128)(2,1)S(1)} reshape(bf16[16384]{0:T(1024)(128)(2,1)} %param.16) | data formatting | bytes 65536 | tf_op jit(solution)/shard_map/reshape | solution.py:183
  33.0 9.2 %all-to-all-done.1.heads = bf16[128,4,128]{2,1,0:T(4,128)(2,1)S(1)} async-done(((bf16[128,4,128]{2,1,0:T(4,128)(2,1)}), bf16[128,4,128]{2,1,0:T(4,128)(2,1)S(1)}, u32[]{:S(2)}, u32[]{:S(2)}) %all-to-all-start.1) | async-done | bytes 131104 | tf_op jit(solution)/shard_map/all_to_all | solution.py:171
  42.1 0.0 copy-start
  42.1 2.9 %copy-done = bf16[208,16384]{1,0:T(8,128)(2,1)S(1)} copy-done((bf16[208,16384]{1,0:T(8,128)(2,1)S(1)}, bf16[208,16384]{1,0:T(8,128)(2,1)}, u32[]{:S(2)}) %copy-start) | copy-done | bytes 6815768
  45.1 0.0 copy-start.1
  45.1 2.9 %copy-done.1 = bf16[208,16384]{1,0:T(8,128)(2,1)S(1)} copy-done((bf16[208,16384]{1,0:T(8,128)(2,1)S(1)}, bf16[208,16384]{1,0:T(8,128)(2,1)}, u32[]{:S(2)}) %copy-start.1) | copy-done | bytes 6815768
  48.0 0.0 copy-start.2
  48.0 2.9 %copy-done.2 = bf16[208,16384]{1,0:T(8,128)(2,1)S(1)} copy-done((bf16[208,16384]{1,0:T(8,128)(2,1)S(1)}, bf16[208,16384]{1,0:T(8,128)(2,1)}, u32[]{:S(2)}) %copy-start.2) | copy-done | bytes 6815768
  50.9 0.0 copy-start.5
  50.9 0.9 %copy-done.5 = bf16[4,16384]{1,0:T(4,128)(2,1)S(1)} copy-done((bf16[4,16384]{1,0:T(4,128)(2,1)S(1)}, bf16[4,16384]{1,0:T(4,128)(2,1)}, u32[]{:S(2)}) %copy-start.5) | copy-done | bytes 131096
  51.8 0.0 copy-start.6
  51.8 5.5 %feed_forward.1 = f32[128,4,128]{2,1,0:T(4,128)} custom-call(bf16[128,4,128]{2,1,0:T(4,128)(2,1)S(1)} %all-to-all-done.1.heads, bf16[4,16384]{1,0:T(4,128)(2,1)S(1)} %copy-done.5, bf16[1,16384]{1,0:T(2,128)(2,1)S(1)} %reshape.15.gain, bf16[208,16384]{1,0:T(8,128)(2,1)S(1)} %copy-done, bf16[208,16384]{1,0:T(8,128)(2,1)S(1)} %copy-done.1, ...), custom_call_target="tpu_custom_call" | custom-call | tf_op jit(solution)/shard_map/feed_forward/pallas_call | solution.py:172
  57.3 4.3 %all-to-all-start.2 = ((f32[128,4,128]{2,1,0:T(4,128)}), f32[128,4,128]{2,1,0:T(4,128)S(1)}, u32[]{:S(2)}, u32[]{:S(2)}) async-start(f32[128,4,128]{2,1,0:T(4,128)} %feed_forward.1), calls=%async_computation.2 | async-start | bytes 524288 | tf_op jit(solution)/shard_map/all_to_all | solution.py:188
  61.6 0.6 copy.12
  62.3 10.5 %all-to-all-done.2.parts = f32[128,4,128]{2,1,0:T(4,128)S(1)} async-done(((f32[128,4,128]{2,1,0:T(4,128)}), f32[128,4,128]{2,1,0:T(4,128)S(1)}, u32[]{:S(2)}, u32[]{:S(2)}) %all-to-all-start.2) | async-done | bytes 262176 | tf_op jit(solution)/shard_map/all_to_all | solution.py:188
  72.7 0.0 copy-done.6
  72.7 0.7 add_shares.1
  (1 shorter events, 0.0 us)
Async XLA Ops:
  0.6 1.6 %copy-start.3 = (bf16[256,16,2,128]{3,2,1,0:T(2,128)(2,1)S(1)}, bf16[256,16,2,128]{3,2,1,0:T(2,128)(2,1)}, u32[]{:S(2)}) copy-start(bf16[256,16,2,128]{3,2,1,0:T(2,128)(2,1)} %param.11) | copy-start | bytes 6291460
  2.2 1.6 %copy-start.4 = (bf16[256,16,2,128]{3,2,1,0:T(2,128)(2,1)S(1)}, bf16[256,16,2,128]{3,2,1,0:T(2,128)(2,1)}, u32[]{:S(2)}) copy-start(bf16[256,16,2,128]{3,2,1,0:T(2,128)(2,1)} %param.12) | copy-start | bytes 6291460
  3.8 0.8 %copy-start.7 = (bf16[4,32,128]{2,1,0:T(8,128)(2,1)S(1)}, bf16[4,32,128]{2,1,0:T(8,128)(2,1)}, u32[]{:S(2)}) copy-start(bf16[4,32,128]{2,1,0:T(8,128)(2,1)} %query.1) | copy-start | bytes 98308
  4.6 0.7 copy-start.8
  5.3 0.7 copy-start.9
  26.2 15.9 %all-to-all-start.1 = ((bf16[128,4,128]{2,1,0:T(4,128)(2,1)}), bf16[128,4,128]{2,1,0:T(4,128)(2,1)S(1)}, u32[]{:S(2)}, u32[]{:S(2)}) async-start(bf16[128,4,128]{2,1,0:T(4,128)(2,1)} %merge_blocks.1), calls=%async_computation.1 | async-start | bytes 262144 | tf_op jit(solution)/shard_map/all_to_all | solution.py:171
  42.1 2.9 %copy-start = (bf16[208,16384]{1,0:T(8,128)(2,1)S(1)}, bf16[208,16384]{1,0:T(8,128)(2,1)}, u32[]{:S(2)}) copy-start(bf16[208,16384]{1,0:T(8,128)(2,1)} %gate_w.1) | copy-start | bytes 20447236
  45.1 2.9 %copy-start.1 = (bf16[208,16384]{1,0:T(8,128)(2,1)S(1)}, bf16[208,16384]{1,0:T(8,128)(2,1)}, u32[]{:S(2)}) copy-start(bf16[208,16384]{1,0:T(8,128)(2,1)} %up_w.1) | copy-start | bytes 20447236
  48.0 2.9 %copy-start.2 = (bf16[208,16384]{1,0:T(8,128)(2,1)S(1)}, bf16[208,16384]{1,0:T(8,128)(2,1)}, u32[]{:S(2)}) copy-start(bf16[208,16384]{1,0:T(8,128)(2,1)} %down_w.1) | copy-start | bytes 20447236
  50.9 0.9 %copy-start.5 = (bf16[4,16384]{1,0:T(4,128)(2,1)S(1)}, bf16[4,16384]{1,0:T(4,128)(2,1)}, u32[]{:S(2)}) copy-start(bf16[4,16384]{1,0:T(4,128)(2,1)} %residual.3) | copy-start | bytes 393220
  51.8 20.9 %copy-start.6 = (bf16[4,16384]{1,0:T(4,128)(2,1)S(1)}, bf16[4,16384]{1,0:T(4,128)(2,1)}, u32[]{:S(2)}) copy-start(bf16[4,16384]{1,0:T(4,128)(2,1)} %residual.3) | copy-start | bytes 393220
  57.3 15.4 %all-to-all-start.2 = ((f32[128,4,128]{2,1,0:T(4,128)}), f32[128,4,128]{2,1,0:T(4,128)S(1)}, u32[]{:S(2)}, u32[]{:S(2)}) async-start(f32[128,4,128]{2,1,0:T(4,128)} %feed_forward.1), calls=%async_computation.2 | async-start | bytes 524288 | tf_op jit(solution)/shard_map/all_to_all | solution.py:188

commit v2 on v1

--- a/solution.py
+++ b/solution.py
@@ -1,5 +1,3 @@
-import functools
-
 import jax
 import jax.numpy as jnp
 from jax import lax
@@ -13,16 +11,31 @@
 MIB = 1 << 20
 NT = (((1,), (1,)), ((), ()))
 PAGES_PER_DOT = 8
-
-
-def attention_kernel(lengths, table, query, keys, values, out, k_vmem, v_vmem, sems):
+PARTS = 4
+CHUNK = 2048
+IN_STEPS = 8
+OUT_STEPS = 4
+
+
+def attention_kernel(
+    lengths_h, table_h, query_h, keys, values, out, lengths, table, query, k_vmem, v_vmem, sems
+):
     rows, heads, width = query.shape
     pages = table.shape[1]
     cells = keys.shape[0] // (rows * pages)
-    k_copy = pltpu.make_async_copy(keys, k_vmem, sems.at[0])
-    v_copy = pltpu.make_async_copy(values, v_vmem, sems.at[1])
-    k_copy.start()
-    v_copy.start()
+    small = [
+        pltpu.make_async_copy(table_h, table, sems.at[0]),
+        pltpu.make_async_copy(lengths_h, lengths, sems.at[1]),
+        pltpu.make_async_copy(query_h, query, sems.at[2]),
+    ]
+    part = keys.shape[0] // PARTS
+    k_copies, v_copies = [], []
+    for i in range(PARTS):
+        at = pl.ds(i * part, part)
+        k_copies.append(pltpu.make_async_copy(keys.at[at], k_vmem.at[at], sems.at[3 + i]))
+        v_copies.append(pltpu.make_async_copy(values.at[at], v_vmem.at[at], sems.at[3 + PARTS + i]))
+    for copy in small + k_copies + v_copies:
+        copy.start()
     first = lax.axis_index("kv") * (pages * cells // 2)
     span = pages * cells
     column = lax.broadcasted_iota(jnp.int32, (heads, span), 1)
@@ -41,7 +54,8 @@
         )
 
     kept = []
-    k_copy.wait()
+    for copy in small + k_copies:
+        copy.wait()
     for row in range(rows):
         q = query[row]
         scores = jnp.concatenate(
@@ -58,7 +72,8 @@
         total = jnp.sum(weights, axis=-1, keepdims=True)
         kept.append(weights.astype(BF16))
         out[:, rows + row, :] = jnp.where(lane < width // 2, top, total)
-    v_copy.wait()
+    for copy in v_copies:
+        copy.wait()
     for row in range(rows):
         summed = jnp.zeros((heads, width), F32)
         for at in range(0, pages, PAGES_PER_DOT):
@@ -84,9 +99,40 @@
     out[...] = jnp.broadcast_to(done[None], out.shape)
 
 
-def feed_kernel(heads, residual, gain, gate_w, up_w, down_w, out, normed, chunk):
+def feed_kernel(
+    heads, residual_h, gain_h, gate_h, up_h, down_h, out, residual, gain, gate_w, up_w, down_w, normed, sems
+):
     count, rows, width = heads.shape
     features = count * width
+    small = [
+        pltpu.make_async_copy(residual_h, residual, sems.at[3, 0]),
+        pltpu.make_async_copy(gain_h, gain, sems.at[3, 1]),
+    ]
+    in_step = features // IN_STEPS
+    out_step = features // OUT_STEPS
+
+    def pieces(source, target, which, steps):
+        step = features // steps
+        copies = []
+        for i in range(steps):
+            at = pl.ds(i * step, step)
+            copies.append(
+                pltpu.make_async_copy(source.at[:, at], target.at[:, at], sems.at[which, i])
+            )
+        return copies
+
+    gate_copies = pieces(gate_h, gate_w, 0, IN_STEPS)
+    up_copies = pieces(up_h, up_w, 1, IN_STEPS)
+    down_copies = pieces(down_h, down_w, 2, OUT_STEPS)
+    for copy in small:
+        copy.start()
+    for i in range(IN_STEPS):
+        gate_copies[i].start()
+        up_copies[i].start()
+    for copy in down_copies:
+        copy.start()
+    for copy in small:
+        copy.wait()
     squares = jnp.zeros((rows, width), F32)
     for i in range(count):
         cols = slice(i * width, (i + 1) * width)
@@ -97,19 +143,25 @@
     for i in range(count):
         cols = slice(i * width, (i + 1) * width)
         hidden = residual[:, cols].astype(F32) + heads[i].astype(F32)
-        normed[:, cols] = (hidden * scale * gain[:, cols].astype(F32)).astype(BF16)
+        normed[:, cols] = (hidden * scale * gain[i : i + 1, :].astype(F32)).astype(BF16)
     units = gate_w.shape[0]
     gate = jnp.zeros((rows, units), F32)
     up = jnp.zeros((rows, units), F32)
-    for at in range(0, features, chunk):
-        x = normed[:, at : at + chunk]
-        gate += lax.dot_general(x, gate_w[:, at : at + chunk], NT, preferred_element_type=F32)
-        up += lax.dot_general(x, up_w[:, at : at + chunk], NT, preferred_element_type=F32)
+    for i in range(IN_STEPS):
+        at = i * in_step
+        x = normed[:, at : at + in_step]
+        gate_copies[i].wait()
+        up_copies[i].wait()
+        gate += lax.dot_general(x, gate_w[:, at : at + in_step], NT, preferred_element_type=F32)
+        up += lax.dot_general(x, up_w[:, at : at + in_step], NT, preferred_element_type=F32)
     activated = (gate / (1.0 + jnp.exp(-gate)) * up).astype(BF16)
-    for at in range(0, features, chunk):
-        mixed = jnp.dot(activated, down_w[:, at : at + chunk], preferred_element_type=F32)
-        for j in range(chunk // width):
-            out[at // width + j] = mixed[:, j * width : (j + 1) * width]
+    for i in range(OUT_STEPS):
+        at = i * out_step
+        down_copies[i].wait()
+        for half in range(at, at + out_step, CHUNK):
+            mixed = jnp.dot(activated, down_w[:, half : half + CHUNK], preferred_element_type=F32)
+            for j in range(CHUNK // width):
+                out[half // width + j] = mixed[:, j * width : (j + 1) * width]
 
 
 def final_kernel(parts, heads, residual, out):
@@ -121,12 +173,11 @@
 
 
 VMEM = pl.BlockSpec(memory_space=pltpu.VMEM)
-SMEM = pl.BlockSpec(memory_space=pltpu.SMEM)
-ANY = pl.BlockSpec(memory_space=pl.ANY)
-
-
-def in_vmem(x):
-    return pltpu.with_memory_space_constraint(x, pltpu.VMEM)
+HBM = pl.BlockSpec(memory_space=pltpu.HBM)
+
+
+def in_hbm(*arrays):
+    return [pltpu.with_memory_space_constraint(x, pltpu.HBM) for x in arrays]
 
 
 def shards(
@@ -149,16 +200,19 @@
     partials = pl.pallas_call(
         attention_kernel,
         out_shape=jax.ShapeDtypeStruct((heads, 2 * rows, width), F32),
-        in_specs=[SMEM, SMEM, VMEM, ANY, ANY],
+        in_specs=[HBM] * 5,
         out_specs=VMEM,
         scratch_shapes=[
+            pltpu.SMEM(seq_lengths.shape, jnp.int32),
+            pltpu.SMEM(block_table.shape, jnp.int32),
+            pltpu.VMEM(query.shape, BF16),
             pltpu.VMEM(keys.shape, BF16),
             pltpu.VMEM(values.shape, BF16),
-            pltpu.SemaphoreType.DMA((2,)),
+            pltpu.SemaphoreType.DMA((3 + 2 * PARTS,)),
         ],
         compiler_params=pltpu.CompilerParams(vmem_limit_bytes=16 * MIB),
         name="attention_partials",
-    )(seq_lengths, block_table, query, keys, values)
+    )(*in_hbm(seq_lengths, block_table, query, keys, values))
     gathered = lax.all_to_all(partials, "kv", 0, 0, tiled=True)
     finished = pl.pallas_call(
         merge_kernel,
@@ -170,20 +224,24 @@
     )(gathered)
     all_heads = lax.all_to_all(finished, ("tp", "kv"), 0, 0, tiled=True)
     mixed = pl.pallas_call(
-        functools.partial(feed_kernel, chunk=2048),
+        feed_kernel,
         out_shape=jax.ShapeDtypeStruct((devices, rows, width), F32),
-        in_specs=[VMEM] * 6,
-        out_specs=VMEM,
-        scratch_shapes=[pltpu.VMEM((rows, devices * width), BF16)],
-        compiler_params=pltpu.CompilerParams(vmem_limit_bytes=16 * MIB),
+        in_specs=[VMEM] + [HBM] * 5,
+        out_specs=VMEM,
+        scratch_shapes=[
+            pltpu.VMEM(residual.shape, BF16),
+            pltpu.VMEM((devices, width), BF16),
+            pltpu.VMEM(gate_weight.shape, BF16),
+            pltpu.VMEM(up_weight.shape, BF16),
+            pltpu.VMEM(down_weight.shape, BF16),
+            pltpu.VMEM((rows, devices * width), BF16),
+            pltpu.SemaphoreType.DMA((4, IN_STEPS)),
+        ],
+        compiler_params=pltpu.CompilerParams(vmem_limit_bytes=32 * MIB),
         name="feed_forward",
     )(
         all_heads,
-        residual,
-        norm_gain.reshape(1, -1),
-        in_vmem(gate_weight),
-        in_vmem(up_weight),
-        in_vmem(down_weight),
+        *in_hbm(residual, norm_gain.reshape(devices, width), gate_weight, up_weight, down_weight),
     )
     sums = lax.all_to_all(mixed, ("kv", "tp"), 0, 0, tiled=True)
     layer_out = pl.pallas_call(

time: 74 us -> 61.7 us (0.83)
  local copies, waits for them, and re-layouts: 16.4 us -> 0.64 us
  blocking collectives: 16.9 us -> 32.6 us
  waiting for transfers between devices: 19.6 us -> 10.5 us
  starting transfers between devices: 10.2 us -> 4.41 us
  Pallas kernels: 9.66 us -> 12.6 us
    all_to_all x0 -> x1, blocking collectives: none -> 15.8 us  [shards(): all_heads = lax.all_to_all(finished, ('tp', 'kv'), 0, 0, tiled=True)]
    unnamed x21 -> x3, local copies, waits for them, and re-layouts: 15.6 us -> 0.62 us
    all_to_all x1 -> x0, waiting for transfers between devices: 9.16 us -> none  [shards(): all_heads = lax.all_to_all(finished, ('tp', 'kv'), 0, 0, tiled=True)]
    all_to_all x1 -> x0, starting transfers between devices: 5.92 us -> none  [shards(): all_heads = lax.all_to_all(finished, ('tp', 'kv'), 0, 0, tiled=True)]
    pallas_call x1, Pallas kernels: 5.49 us -> 8.34 us  [shards(): pl.pallas_call(feed_kernel, out_shape=jax.ShapeDtypeStruct((devices, rows...]
    reshape x1 -> x0, local copies, waits for them, and re-layouts: 0.8 us -> none  [shards(): norm_gain.reshape(1, -1)]
    pallas_call x1, Pallas kernels: 2.61 us -> 3.36 us  [shards(): pl.pallas_call(attention_kernel, out_shape=jax.ShapeDtypeStruct((heads, 2...]
  transfers between devices with their start and end apart: 2 -> 1, of which waited for: 2 -> 1; matrix products, arithmetic and copies ran while one was open for 2% -> 1% of each run, Pallas kernels for 0% -> 0%
where the time goes in v2:
time: 61.7 us; the launch traced here: 61.4 us
  blocking collectives  32.6 us (53%)
  Pallas kernels  12.6 us (20%)
  waiting for transfers between devices  10.5 us (17%)
  starting transfers between devices  4.41 us (7%)
  between operations  0.68 us (1%)
  local copies, waits for them, and re-layouts  0.64 us (1%)
    all_to_all x1, blocking collectives, shards(): gathered = lax.all_to_all(partials, 'kv', 0, 0, tiled=True)  16.9 us
    all_to_all x1, blocking collectives, shards(): all_heads = lax.all_to_all(finished, ('tp', 'kv'), 0, 0, tiled=True)  15.8 us
    all_to_all x1, waiting for transfers between devices, shards(): sums = lax.all_to_all(mixed, ('kv', 'tp'), 0, 0, tiled=True)  10.5 us
    pallas_call x1, Pallas kernels, shards(): pl.pallas_call(feed_kernel, out_shape=jax.ShapeDtypeStruct((devices, rows...  8.34 us
    all_to_all x1, starting transfers between devices, shards(): sums = lax.all_to_all(mixed, ('kv', 'tp'), 0, 0, tiled=True)  4.41 us
    pallas_call x1, Pallas kernels, shards(): pl.pallas_call(attention_kernel, out_shape=jax.ShapeDtypeStruct((heads, 2...  3.36 us
  transfers between devices with their start and end apart: 1, of which 1 were waited for; matrix products, arithmetic and copies ran while one was open for 1% of the time, Pallas kernels for 0%

profile of v2, /device:TPU:1, one launch (start us, length us, event | category | flops | bytes accessed | tf_op | source)
XLA Modules:
  0.0 61.4 jit_solution(9203330516461312898)
XLA Ops:
  0.6 3.4 %attention_partials.1 = f32[32,8,128]{2,1,0:T(8,128)S(1)} custom-call(s32[4]{0:T(128)} %lengths_h.1, s32[4,64]{1,0:T(4,128)} %table_h.1, bf16[4,32,128]{2,1,0:T(8,128)(2,1)} %query_h.1, bf16[8192,128]{1,0:T(8,128)(2,1)} %bitcast.5, bf16[8192,128]{1,0:T(8,128)(2,1)} %bitcast.6), custom_call_target="tpu_custom_call" | custom-call | tf_op jit(solution)/shard_map/attention_partials/pallas_call | solution.py:200
  4.0 16.9 %all_to_all.15.parts = f32[32,8,128]{2,1,0:T(8,128)S(1)} all-to-all(f32[32,8,128]{2,1,0:T(8,128)S(1)} %attention_partials.1), channel_id=1, replica_groups=mesh['kv'=32,'tp'=4] {'kv'}, dimensions={0} | all-to-all | bytes 262144 | tf_op jit(solution)/shard_map/all_to_all | solution.py:216
  20.9 0.2 merge_blocks.1
  21.1 15.8 %all_to_all.16.heads = bf16[128,4,128]{2,1,0:T(4,128)(2,1)S(1)} all-to-all(bf16[128,4,128]{2,1,0:T(4,128)(2,1)S(1)} %merge_blocks.1), channel_id=1, replica_groups=mesh['kv'=32,'tp'=4] {'tp','kv'}, dimensions={0} | all-to-all | bytes 262144 | tf_op jit(solution)/shard_map/all_to_all | solution.py:225
  36.9 0.0 copy-start
  36.9 8.3 %feed_forward.1 = f32[128,4,128]{2,1,0:T(4,128)} custom-call(bf16[128,4,128]{2,1,0:T(4,128)(2,1)S(1)} %all_to_all.16.heads, bf16[4,16384]{1,0:T(4,128)(2,1)} %residual.1, bf16[128,128]{1,0:T(8,128)(2,1)} %bitcast.7, bf16[208,16384]{1,0:T(8,128)(2,1)} %gate_h.1, bf16[208,16384]{1,0:T(8,128)(2,1)} %up_h.1, bf16[208,16384]{1,0:T(8,128)(2,1)} %down_h.1), custom_call_target="tpu_custom_call" | custom-call | tf_op jit(solution)/shard_map/feed_forward/pallas_call | solution.py:226
  45.2 4.4 %all-to-all-start.2 = ((f32[128,4,128]{2,1,0:T(4,128)}), f32[128,4,128]{2,1,0:T(4,128)S(1)}, u32[]{:S(2)}, u32[]{:S(2)}) async-start(f32[128,4,128]{2,1,0:T(4,128)} %feed_forward.1), calls=%async_computation.2 | async-start | bytes 524288 | tf_op jit(solution)/shard_map/all_to_all | solution.py:246
  49.6 0.6 %copy.12 = bf16[4,32,128]{2,1,0:T(8,128)(2,1)} copy(bf16[4,32,128]{2,0,1:T(4,128)(2,1)S(1)} %dynamic-slice_bitcast_fusion) | data formatting | bytes 65536
  50.3 10.5 %all-to-all-done.2.parts = f32[128,4,128]{2,1,0:T(4,128)S(1)} async-done(((f32[128,4,128]{2,1,0:T(4,128)}), f32[128,4,128]{2,1,0:T(4,128)S(1)}, u32[]{:S(2)}, u32[]{:S(2)}) %all-to-all-start.2) | async-done | bytes 262176 | tf_op jit(solution)/shard_map/all_to_all | solution.py:246
  60.7 0.0 copy-done
  60.7 0.7 %add_shares.1 = bf16[4,128]{1,0:T(4,128)(2,1)} custom-call(f32[128,4,128]{2,1,0:T(4,128)S(1)} %all-to-all-done.2.parts, bf16[128,4,128]{2,1,0:T(4,128)(2,1)S(1)} %all_to_all.16.heads, bf16[4,16384]{1,0:T(4,128)(2,1)S(1)} %copy-done), custom_call_target="tpu_custom_call" | custom-call | tf_op jit(solution)/shard_map/add_shares/pallas_call | solution.py:247
  (1 shorter events, 0.0 us)
Async XLA Ops:
  36.9 23.9 %copy-start = (bf16[4,16384]{1,0:T(4,128)(2,1)S(1)}, bf16[4,16384]{1,0:T(4,128)(2,1)}, u32[]{:S(2)}) copy-start(bf16[4,16384]{1,0:T(4,128)(2,1)} %residual.1) | copy-start | bytes 393220
  45.2 15.5 %all-to-all-start.2 = ((f32[128,4,128]{2,1,0:T(4,128)}), f32[128,4,128]{2,1,0:T(4,128)S(1)}, u32[]{:S(2)}, u32[]{:S(2)}) async-start(f32[128,4,128]{2,1,0:T(4,128)} %feed_forward.1), calls=%async_computation.2 | async-start | bytes 524288 | tf_op jit(solution)/shard_map/all_to_all | solution.py:246

commit v3 on v2

v3 whole, which is shorter than its diff:
```python
import functools

import jax
import jax.numpy as jnp
from jax import lax
from jax.experimental import pallas as pl
from jax.experimental.pallas import tpu as pltpu
from jax.sharding import Mesh
from jax.sharding import PartitionSpec as P

NEG = -1e30
F32 = jnp.float32
BF16 = jnp.bfloat16
MIB = 1 << 20
NT = (((1,), (1,)), ((), ()))
PAGES_PER_DOT = 8
PARTS = 4
CHUNK = 2048
IN_STEPS = 8
OUT_STEPS = 4


def kv_index():
    return lax.axis_index("chip") * lax.axis_size("core") + lax.axis_index("core")


def attention_kernel(
    lengths_h, table_h, query_h, keys, values, keep, send, lengths, table, query, k_vmem, v_vmem, sems
):
    rows, heads, width = query.shape
    pages = table.shape[1]
    cells = keys.shape[0] // (rows * pages)
    small = [
        pltpu.make_async_copy(table_h, table, sems.at[0]),
        pltpu.make_async_copy(lengths_h, lengths, sems.at[1]),
        pltpu.make_async_copy(query_h, query, sems.at[2]),
    ]
    part = keys.shape[0] // PARTS
    k_copies, v_copies = [], []
    for i in range(PARTS):
        at = pl.ds(i * part, part)
        k_copies.append(pltpu.make_async_copy(keys.at[at], k_vmem.at[at], sems.at[3 + i]))
        v_copies.append(pltpu.make_async_copy(values.at[at], v_vmem.at[at], sems.at[3 + PARTS + i]))
    for copy in small + k_copies + v_copies:
        copy.start()
    first = kv_index() * (pages * cells // 2)
    span = pages * cells
    column = lax.broadcasted_iota(jnp.int32, (heads, span), 1)
    head = lax.broadcasted_iota(jnp.int32, (heads, span), 0)
    own = (column % 2) == (head // (heads // 2))
    position = jnp.where(own, first + column // 2, jnp.int32(2**30))
    lane = lax.broadcasted_iota(jnp.int32, (heads, width), 1)
    half = heads // 2
    core = lax.axis_index("core")

    def put(row, block):
        low, high = block[:half], block[half:]
        keep[:, row, :] = jnp.where(core == 0, low, high)
        send[:, row, :] = jnp.where(core == 0, high, low)

    def block(ref, row, at):
        return jnp.concatenate(
            [
                ref[pl.ds(pl.multiple_of(table[row, at + i] * cells, cells), cells), :]
                for i in range(PAGES_PER_DOT)
            ],
            axis=0,
        )

    kept = []
    for copy in small + k_copies:
        copy.wait()
    for row in range(rows):
        q = query[row]
        scores = jnp.concatenate(
            [
                lax.dot_general(q, block(k_vmem, row, at), NT, preferred_element_type=F32)
                for at in range(0, pages, PAGES_PER_DOT)
            ],
            axis=1,
        ) * (width**-0.5)
        active = position < lengths[row]
        masked = jnp.where(active, scores, NEG)
        top = jnp.max(masked, axis=-1, keepdims=True)
        weights = jnp.where(active, jnp.exp(masked - top), 0.0)
        total = jnp.sum(weights, axis=-1, keepdims=True)
        kept.append(weights.astype(BF16))
        put(rows + row, jnp.where(lane < width // 2, top, total))
    for copy in v_copies:
        copy.wait()
    for row in range(rows):
        summed = jnp.zeros((heads, width), F32)
        for at in range(0, pages, PAGES_PER_DOT):
            summed += jnp.dot(
                kept[row][:, at * cells : (at + PAGES_PER_DOT) * cells],
                block(v_vmem, row, at),
                preferred_element_type=F32,
            )
        put(row, summed)


def pack(out, means, log_total):
    heads = len(means)
    copies = out.shape[0]
    for h in range(heads):
        mean = means[h].astype(BF16)
        for i in range(copies):
            out[i, h] = mean
    first = log_total.astype(BF16).astype(F32)
    second = (log_total - first).astype(BF16).astype(F32)
    third = log_total - first - second
    rest = jnp.zeros((first.shape[0], out.shape[-1] - 3 * heads), F32)
    terms = jnp.concatenate([first, second, third, rest], axis=1).astype(BF16)
    for i in range(copies):
        out[i, heads] = terms


def merge_cores_kernel(keep, received, out):
    heads, double, width = keep.shape
    rows = double // 2
    mine, theirs = keep[...], received[...]

    def stats(block):
        return block[:, rows:, 0:1], block[:, rows:, width // 2 : width // 2 + 1]

    top_a, total_a = stats(mine)
    top_b, total_b = stats(theirs)
    top = jnp.maximum(top_a, top_b)
    factor_a, factor_b = jnp.exp(top_a - top), jnp.exp(top_b - top)
    total = factor_a * total_a + factor_b * total_b
    summed = factor_a * mine[:, :rows, :] + factor_b * theirs[:, :rows, :]
    live = total > 0.0
    safe = jnp.where(live, total, 1.0)
    mean = jnp.where(live, summed / safe, 0.0)
    log_total = jnp.where(live, top + jnp.log(safe), NEG)
    shape = (heads, rows, width)
    here = lax.broadcasted_iota(jnp.int32, shape, 2) == lax.broadcasted_iota(jnp.int32, shape, 0)
    pack(out, list(mean), jnp.sum(jnp.where(here, log_total, 0.0), axis=0)[:, :heads])


def merge_chips_kernel(parts, out):
    count = parts.shape[0]
    heads = parts.shape[1] - 1
    logs = []
    for i in range(count):
        terms = parts[i, heads].astype(F32)
        logs.append(terms[:, :heads] + terms[:, heads : 2 * heads] + terms[:, 2 * heads : 3 * heads])
    top = functools.reduce(jnp.maximum, logs)
    factors = [jnp.exp(log - top) for log in logs]
    total = functools.reduce(jnp.add, factors)
    shares = [factor / total for factor in factors]
    for h in range(heads):
        out[h] = functools.reduce(
            jnp.add, [shares[i][:, h : h + 1] * parts[i, h].astype(F32) for i in range(count)]
        ).astype(BF16)


def join_kernel(*refs):
    for i in range(refs[-1].shape[0]):
        refs[-1][i] = refs[i][...]


def feed_kernel(
    mine,
    theirs,
    residual,
    gain,
    gate_w,
    up_h,
    down_h,
    out,
    share_out,
    up_w,
    down_w,
    hidden,
    normed,
    sems,
):
    groups, half, rows, width = mine.shape
    count = groups * half * 2
    features = count * width
    kv, tp = kv_index(), lax.axis_index("tp")
    in_step = features // IN_STEPS
    out_step = features // OUT_STEPS

    def pieces(source, target, which, steps):
        step = features // steps
        copies = []
        for i in range(steps):
            at = pl.ds(i * step, step)
            copies.append(
                pltpu.make_async_copy(source.at[:, at], target.at[:, at], sems.at[which, i])
            )
        return copies

    up_copies = pieces(up_h, up_w, 0, IN_STEPS)
    down_copies = pieces(down_h, down_w, 1, OUT_STEPS)
    for copy in up_copies + down_copies:
        copy.start()
    squares = jnp.zeros((rows, width), F32)
    for part, core in ((mine, kv % 2), (theirs, 1 - kv % 2)):
        for distance in range(groups):
            base = ((tp + distance) % groups) * (2 * half) + core * half
            for i in range(half):
                cols = pl.ds(pl.multiple_of((base + i) * width, width), width)
                value = residual[:, cols].astype(F32) + part[distance, i].astype(F32)
                hidden[base + i] = value
                squares += value * value
    mean_square = jnp.sum(squares, axis=-1, keepdims=True) / features
    scale = lax.rsqrt(mean_square + 1e-05)
    for i in range(count):
        cols = slice(i * width, (i + 1) * width)
        normed[:, cols] = (hidden[i] * scale * gain[i : i + 1, :].astype(F32)).astype(BF16)
    share_out[...] = hidden[kv * groups + tp]
    units = gate_w.shape[0]
    gate = jnp.zeros((rows, units), F32)
    up = jnp.zeros((rows, units), F32)
    for i in range(IN_STEPS):
        at = i * in_step
        x = normed[:, at : at + in_step]
        up_copies[i].wait()
        gate += lax.dot_general(x, gate_w[:, at : at + in_step], NT, preferred_element_type=F32)
        up += lax.dot_general(x, up_w[:, at : at + in_step], NT, preferred_element_type=F32)
    activated = (gate / (1.0 + jnp.exp(-gate)) * up).astype(BF16)
    for i in range(OUT_STEPS):
        at = i * out_step
        down_copies[i].wait()
        for half in range(at, at + out_step, CHUNK):
            mixed = jnp.dot(activated, down_w[:, half : half + CHUNK], preferred_element_type=F32)
            for j in range(CHUNK // width):
                out[half // width + j] = mixed[:, j * width : (j + 1) * width]


def load_kernel(after, *refs):
    count = len(refs) // 2
    sems = refs[2 * count]
    copies = []
    for i in range(count):
        copies.append(pltpu.make_async_copy(refs[i], refs[count + i], sems.at[i]))
    for copy in copies:
        copy.start()
    for copy in copies:
        copy.wait()


def load(after, *arrays):
    moved = sum(2 * x.size for x in arrays)
    return pl.pallas_call(
        load_kernel,
        out_shape=[pltpu.VMEM(x.shape, BF16) for x in arrays],
        in_specs=[VMEM] + [HBM] * len(arrays),
        out_specs=[VMEM] * len(arrays),
        scratch_shapes=[pltpu.SemaphoreType.DMA((len(arrays),))],
        compiler_params=pltpu.CompilerParams(vmem_limit_bytes=16 * MIB),
        cost_estimate=pl.CostEstimate(flops=0, bytes_accessed=moved, transcendentals=0),
        name="load_weights",
    )(after, *in_hbm(*arrays))


def own_heads_kernel(finished, theirs, share, out):
    half, rows, width = finished.shape
    first = lax.axis_index("core") == 0
    mine, other = finished[...].astype(F32), theirs[0].astype(F32)
    low = jnp.where(first, mine, other)
    high = jnp.where(first, other, mine)
    for row in range(rows):
        out[row, :half] = low[:, row, :].astype(BF16)
        out[row, half:] = high[:, row, :].astype(BF16)


def final_kernel(parts, share, out):
    out[...] = (share[...] + jnp.sum(parts[...], axis=0)).astype(BF16)


VMEM = pl.BlockSpec(memory_space=pltpu.VMEM)
HBM = pl.BlockSpec(memory_space=pltpu.HBM)


def in_hbm(*arrays):
    return [pltpu.with_memory_space_constraint(x, pltpu.HBM) for x in arrays]


def shards(
    query,
    key_cache,
    value_cache,
    seq_lengths,
    block_table,
    residual,
    norm_gain,
    gate_weight,
    up_weight,
    down_weight,
):
    rows, heads, width = query.shape
    keys = key_cache.reshape(-1, width)
    values = value_cache.reshape(-1, width)
    kv_size, tp_size = lax.axis_size("chip") * lax.axis_size("core"), lax.axis_size("tp")
    devices = kv_size * tp_size
    half = heads // 2
    small = pltpu.CompilerParams(vmem_limit_bytes=16 * MIB)
    block_f32 = jax.ShapeDtypeStruct((half, 2 * rows, width), F32)
    packed = jax.ShapeDtypeStruct((lax.axis_size("chip"), half + 1, rows, width), BF16)
    keep, send = pl.pallas_call(
        attention_kernel,
        out_shape=[block_f32] * 2,
        in_specs=[HBM] * 5,
        out_specs=[VMEM] * 2,
        scratch_shapes=[
            pltpu.SMEM(seq_lengths.shape, jnp.int32),
            pltpu.SMEM(block_table.shape, jnp.int32),
            pltpu.VMEM(query.shape, BF16),
            pltpu.VMEM(keys.shape, BF16),
            pltpu.VMEM(values.shape, BF16),
            pltpu.SemaphoreType.DMA((3 + 2 * PARTS,)),
        ],
        compiler_params=small,
        name="attention_partials",
    )(*in_hbm(seq_lengths, block_table, query, keys, values))

    def call(kernel, out_shape, name, *operands):
        return pl.pallas_call(
            kernel,
            out_shape=out_shape,
            in_specs=[VMEM] * len(operands),
            out_specs=VMEM,
            compiler_params=small,
            name=name,
        )(*operands)

    def ring(x):
        one, three, two = (
            lax.ppermute(x, "tp", [(i, (i - distance) % tp_size) for i in range(tp_size)])
            for distance in (1, 3, 2)
        )
        return one, two, three

    swap = [(0, 1), (1, 0)]
    block = call(
        merge_cores_kernel, packed, "merge_cores", keep, lax.ppermute(send, "core", swap)
    )
    blocks = lax.all_to_all(block, "chip", 0, 0, tiled=True)
    finished = call(
        merge_chips_kernel,
        jax.ShapeDtypeStruct((half, rows, width), BF16),
        "merge_chips",
        blocks,
    )
    around = ring(finished)
    gate, res, gain = load(
        finished, gate_weight, residual, norm_gain.reshape(devices, width)
    )
    mine = call(
        join_kernel,
        jax.ShapeDtypeStruct((tp_size, half, rows, width), BF16),
        "join_heads",
        finished,
        *around,
        gain,
    )
    theirs = lax.ppermute(mine, "core", swap)
    mixed, share = pl.pallas_call(
        feed_kernel,
        out_shape=[
            jax.ShapeDtypeStruct((devices, rows, width), F32),
            jax.ShapeDtypeStruct((rows, width), F32),
        ],
        in_specs=[VMEM] * 5 + [HBM] * 2,
        out_specs=[VMEM] * 2,
        scratch_shapes=[
            pltpu.VMEM(up_weight.shape, BF16),
            pltpu.VMEM(down_weight.shape, BF16),
            pltpu.VMEM((devices, rows, width), F32),
            pltpu.VMEM((rows, devices * width), BF16),
            pltpu.SemaphoreType.DMA((2, IN_STEPS)),
        ],
        compiler_params=pltpu.CompilerParams(vmem_limit_bytes=32 * MIB),
        name="feed_forward",
    )(
        mine,
        theirs,
        res,
        gain,
        gate,
        *in_hbm(up_weight, down_weight),
    )
    sums = lax.all_to_all(mixed, ("chip", "core", "tp"), 0, 0, tiled=True)
    layer_out = call(
        final_kernel, jax.ShapeDtypeStruct((rows, width), BF16), "add_shares", sums, share
    )
    attention = call(
        own_heads_kernel,
        jax.ShapeDtypeStruct(query.shape, BF16),
        "own_heads",
        finished,
        theirs,
        share,
    )
    return layer_out, attention


def solution(mesh):
    devices = mesh.devices
    split = Mesh(devices.reshape(-1, 2, devices.shape[1]), ("chip", "core", "tp"))
    kv = ("chip", "core")
    every = ("chip", "core", "tp")
    placed = (
        P(None, "tp", None),
        P(kv, None, "tp", None),
        P(kv, None, "tp", None),
        P(),
        P(None, kv),
        P(),
        P(),
        P(every, None),
        P(every, None),
        P(every, None),
    )
    return jax.shard_map(
        shards,
        mesh=split,
        in_specs=placed,
        out_specs=(P(None, every), P(None, "tp", None)),
        check_vma=False,
    )
```

time: 61.7 us -> 58 us (0.940)
  blocking collectives: 32.6 us -> 15.8 us
  starting transfers between devices: 4.41 us -> 13.2 us
  Pallas kernels: 12.6 us -> 15.9 us
  waiting for transfers between devices: 10.5 us -> 12.3 us
  local copies, waits for them, and re-layouts: 0.64 us -> 0 us
    all_to_all x2 -> x1, blocking collectives: 32.6 us -> 15.8 us  [shards(): blocks = lax.all_to_all(block, 'chip', 0, 0, tiled=True)]
    ppermute x0 -> x5, starting transfers between devices: none -> 8.96 us  [the longest x3 5.05 us: ring(): lax.ppermute(x, 'tp', [(i, (i - distance) % tp_size) for i in range(tp_si...]
    pallas_call x4 -> x8, Pallas kernels: 12.6 us -> 15.9 us  [the longest x1 7.43 us: shards(): pl.pallas_call(feed_kernel, out_shape=[jax.ShapeDtypeStruct((devices, row...]
    ppermute x0 -> x5, waiting for transfers between devices: none -> 1.81 us  [the longest x1 0.9 us: shards(): lax.ppermute(send, 'core', swap)]
    unnamed x3 -> x0, local copies, waits for them, and re-layouts: 0.62 us -> none
  transfers between devices with their start and end apart: 1 -> 6, of which waited for: 1 -> 3; matrix products, arithmetic and copies ran while one was open for 1% -> 0% of each run, Pallas kernels for 0% -> 6%
where the time goes in v3:
time: 58 us; the launch traced here: 57.8 us
  Pallas kernels  15.9 us (27%)
  blocking collectives  15.8 us (27%)
  starting transfers between devices  13.2 us (23%)
  waiting for transfers between devices  12.3 us (21%)
  between operations  0.71 us (1%)
    all_to_all x1, blocking collectives, shards(): blocks = lax.all_to_all(block, 'chip', 0, 0, tiled=True)  15.8 us
    all_to_all x1, waiting for transfers between devices, shards(): sums = lax.all_to_all(mixed, ('chip', 'core', 'tp'), 0, 0, tiled=True)  10.4 us
    pallas_call x1, Pallas kernels, shards(): pl.pallas_call(feed_kernel, out_shape=[jax.ShapeDtypeStruct((devices, row...  7.43 us
    ppermute x3, starting transfers between devices, ring(): lax.ppermute(x, 'tp', [(i, (i - distance) % tp_size) for i in range(tp_si...  5.05 us
    all_to_all x1, starting transfers between devices, shards(): sums = lax.all_to_all(mixed, ('chip', 'core', 'tp'), 0, 0, tiled=True)  4.21 us
    pallas_call x1, Pallas kernels, shards(): pl.pallas_call(attention_kernel, out_shape=[block_f32] * 2, in_specs=[HBM...  3.35 us
    pallas_call x1, Pallas kernels, load(): pl.pallas_call(load_kernel, out_shape=[pltpu.VMEM(x.shape, BF16) for x in...  2.96 us
    ppermute x1, starting transfers between devices, shards(): theirs = lax.ppermute(mine, 'core', swap)  2.42 us
  transfers between devices with their start and end apart: 6, of which 3 were waited for; matrix products, arithmetic and copies ran while one was open for 0% of the time, Pallas kernels for 6%

profile of v3, /device:TPU:1, one launch (start us, length us, event | category | flops | bytes accessed | tf_op | source)
XLA Modules:
  0.0 57.8 jit_solution(6523090905036671171)
XLA Ops:
  0.6 3.3 %attention_partials.1 = (f32[16,8,128]{2,1,0:T(8,128)S(1)}, f32[16,8,128]{2,1,0:T(8,128)S(1)}) custom-call(s32[4]{0:T(128)} %lengths_h.1, s32[4,64]{1,0:T(4,128)} %table_h.1, bf16[4,32,128]{2,1,0:T(8,128)(2,1)} %query_h.1, bf16[8192,128]{1,0:T(8,128)(2,1)} %bitcast.3, bf16[8192,128]{1,0:T(8,128)(2,1)} %bitcast.4), custom_call_target="tpu_custom_call" | custom-call | tf_op jit(solution)/shard_map/attention_partials/pallas_call | solution.py:304
  4.0 1.5 %collective-permute-start = (f32[16,8,128]{2,1,0:T(8,128)S(1)}, f32[16,8,128]{2,1,0:T(8,128)S(1)}, u32[]{:S(2)}, u32[]{:S(2)}) collective-permute-start(f32[16,8,128]{2,1,0:T(8,128)S(1)} %get-tuple-element.10), channel_id=1, source_target_pairs={{0,4},{4,0},{1,5},{5,1},{2,6},{6,2},{3,7},{7,3},{8,12},{12,8},{9,1... | collective-permute-start | bytes 196616 | tf_op jit(solution)/shard_map/ppermute | solution.py:340
  5.5 0.9 %collective-permute-done.received = f32[16,8,128]{2,1,0:T(8,128)S(1)} collective-permute-done((f32[16,8,128]{2,1,0:T(8,128)S(1)}, f32[16,8,128]{2,1,0:T(8,128)S(1)}, u32[]{:S(2)}, u32[]{:S(2)}) %collective-permute-start) | collective-permute-done | bytes 65568 | tf_op jit(solution)/shard_map/ppermute | solution.py:340
  6.4 0.3 merge_cores.1
  6.7 15.8 %all_to_all.10.parts = bf16[16,17,4,128]{3,2,1,0:T(4,128)(2,1)S(1)} all-to-all(bf16[16,17,4,128]{3,2,1,0:T(4,128)(2,1)S(1)} %merge_cores.1), channel_id=1, replica_groups=mesh['chip'=16,'core'=2,'tp'=4] {'chip'}, dimensions={0} | all-to-all | bytes 557056 | tf_op jit(solution)/shard_map/all_to_all | solution.py:342
  22.5 0.5 merge_chips.1.after.refs_0_.finished
  23.0 1.4 %collective-permute-start.3 = (bf16[16,4,128]{2,1,0:T(4,128)(2,1)S(1)}, bf16[16,4,128]{2,1,0:T(4,128)(2,1)S(1)}, u32[]{:S(2)}, u32[]{:S(2)}) collective-permute-start(bf16[16,4,128]{2,1,0:T(4,128)(2,1)S(1)} %merge_chips.1.after.refs_0_.finished), channel_id=1, source_target_pairs={{0,1},{1,2},{2,3},{3,0},{4,5},{5,6},{6,7},{7,4},{8,9},{9,10},{10,1... | collective-permute-start | bytes 49160 | tf_op jit(solution)/shard_map/ppermute | solution.py:333
  24.3 2.6 %collective-permute-start.2 = (bf16[16,4,128]{2,1,0:T(4,128)(2,1)S(1)}, bf16[16,4,128]{2,1,0:T(4,128)(2,1)S(1)}, u32[]{:S(2)}, u32[]{:S(2)}) collective-permute-start(bf16[16,4,128]{2,1,0:T(4,128)(2,1)S(1)} %merge_chips.1.after.refs_0_.finished), channel_id=1, source_target_pairs={{0,2},{1,3},{2,0},{3,1},{4,6},{5,7},{6,4},{7,5},{8,10},{9,11},{10,... | collective-permute-start | bytes 49160 | tf_op jit(solution)/shard_map/ppermute | solution.py:333
  26.9 1.1 %collective-permute-start.1 = (bf16[16,4,128]{2,1,0:T(4,128)(2,1)S(1)}, bf16[16,4,128]{2,1,0:T(4,128)(2,1)S(1)}, u32[]{:S(2)}, u32[]{:S(2)}) collective-permute-start(bf16[16,4,128]{2,1,0:T(4,128)(2,1)S(1)} %merge_chips.1.after.refs_0_.finished), channel_id=1, source_target_pairs={{0,3},{1,0},{2,1},{3,2},{4,7},{5,4},{6,5},{7,6},{8,11},{9,8},{10,9... | collective-permute-start | bytes 49160 | tf_op jit(solution)/shard_map/ppermute | solution.py:333
  28.0 3.0 %load_weights.1 = (bf16[208,16384]{1,0:T(8,128)(2,1)S(1)}, bf16[4,16384]{1,0:T(4,128)(2,1)S(1)}, bf16[128,128]{1,0:T(8,128)(2,1)S(1)}) custom-call(bf16[16,4,128]{2,1,0:T(4,128)(2,1)S(1)} %merge_chips.1.after.refs_0_.finished, bf16[208,16384]{1,0:T(8,128)(2,1)} %refs_0_.1, bf16[4,16384]{1,0:T(4,128)(2,1)} %refs_1_.1, bf16[128,128]{1,0:T(8,128)(2,1)} %bitcast.5), custom_call_target="tpu_custom_call" | custom-call | bytes 6979584 | tf_op jit(solution)/shard_map/load_weights/pallas_call | solution.py:248
  31.0 0.0 collective-permute-done.3.refs_3_
  31.0 0.0 collective-permute-done.2.refs_2_
  31.0 0.0 collective-permute-done.1.refs_1_
  31.0 2.4 %collective-permute-start.4 = (bf16[4,16,4,128]{3,2,1,0:T(4,128)(2,1)S(1)}, bf16[4,16,4,128]{3,2,1,0:T(4,128)(2,1)S(1)}, u32[]{:S(2)}, u32[]{:S(2)}) collective-permute-start(bf16[4,16,4,128]{3,2,1,0:T(4,128)(2,1)S(1)} %join_heads.1.mine), channel_id=1, source_target_pairs={{0,4},{4,0},{1,5},{5,1},{2,6},{6,2},{3,7},{7,3},{8,12},{12,8},{9,1... | collective-permute-start | bytes 196616 | tf_op jit(solution)/shard_map/ppermute | solution.py:361
  33.4 0.9 %collective-permute-done.4.theirs = bf16[4,16,4,128]{3,2,1,0:T(4,128)(2,1)S(1)} collective-permute-done((bf16[4,16,4,128]{3,2,1,0:T(4,128)(2,1)S(1)}, bf16[4,16,4,128]{3,2,1,0:T(4,128)(2,1)S(1)}, u32[]{:S(2)}, u32[]{:S(2)}) %collective-permute-start.4) | collective-permute-done | bytes 65568 | tf_op jit(solution)/shard_map/ppermute | solution.py:361
  34.4 7.4 %feed_forward.1 = (f32[128,4,128]{2,1,0:T(4,128)}, f32[4,128]{1,0:T(4,128)S(1)}) custom-call(bf16[4,16,4,128]{3,2,1,0:T(4,128)(2,1)S(1)} %join_heads.1.mine, bf16[4,16,4,128]{3,2,1,0:T(4,128)(2,1)S(1)} %collective-permute-done.4.theirs, bf16[4,16384]{1,0:T(4,128)(2,1)S(1)} %get-tuple-element.12.residual, ...), custom_call_target="tpu_custom_call" | custom-call | tf_op jit(solution)/shard_map/feed_forward/pallas_call | solution.py:362
  41.8 4.2 %all-to-all-start.1 = ((f32[128,4,128]{2,1,0:T(4,128)}), f32[128,4,128]{2,1,0:T(4,128)S(1)}, u32[]{:S(2)}, u32[]{:S(2)}) async-start(f32[128,4,128]{2,1,0:T(4,128)} %get-tuple-element.14), calls=%async_computation.1 | async-start | bytes 524288 | tf_op jit(solution)/shard_map/all_to_all | solution.py:387
  46.0 0.7 %own_heads.1 = bf16[4,32,128]{2,1,0:T(8,128)(2,1)} custom-call(bf16[16,4,128]{2,1,0:T(4,128)(2,1)S(1)} %merge_chips.1.after.refs_0_.finished, bf16[4,16,4,128]{3,2,1,0:T(4,128)(2,1)S(1)} %collective-permute-done.4.theirs, f32[4,128]{1,0:T(4,128)S(1)} %get-tuple-element.15.share), custom_call_target="tpu_custom_call" | custom-call | tf_op jit(solution)/shard_map/own_heads/pallas_call | solution.py:322
  46.7 10.4 %all-to-all-done.1.parts = f32[128,4,128]{2,1,0:T(4,128)S(1)} async-done(((f32[128,4,128]{2,1,0:T(4,128)}), f32[128,4,128]{2,1,0:T(4,128)S(1)}, u32[]{:S(2)}, u32[]{:S(2)}) %all-to-all-start.1) | async-done | bytes 262176 | tf_op jit(solution)/shard_map/all_to_all | solution.py:387
  57.1 0.7 %add_shares.1 = bf16[4,128]{1,0:T(4,128)(2,1)} custom-call(f32[128,4,128]{2,1,0:T(4,128)S(1)} %all-to-all-done.1.parts, f32[4,128]{1,0:T(4,128)S(1)} %get-tuple-element.15.share), custom_call_target="tpu_custom_call" | custom-call | tf_op jit(solution)/shard_map/add_shares/pallas_call | solution.py:322
  (1 shorter events, 0.0 us)
Async XLA Ops:
  4.0 2.4 %collective-permute-start = (f32[16,8,128]{2,1,0:T(8,128)S(1)}, f32[16,8,128]{2,1,0:T(8,128)S(1)}, u32[]{:S(2)}, u32[]{:S(2)}) collective-permute-start(f32[16,8,128]{2,1,0:T(8,128)S(1)} %get-tuple-element.10), channel_id=1, source_target_pairs={{0,4},{4,0},{1,5},{5,1},{2,6},{6,2},{3,7},{7,3},{8,12},{12,8},{9,1... | collective-permute-start | bytes 196616 | tf_op jit(solution)/shard_map/ppermute | solution.py:340
  23.0 8.0 %collective-permute-start.3 = (bf16[16,4,128]{2,1,0:T(4,128)(2,1)S(1)}, bf16[16,4,128]{2,1,0:T(4,128)(2,1)S(1)}, u32[]{:S(2)}, u32[]{:S(2)}) collective-permute-start(bf16[16,4,128]{2,1,0:T(4,128)(2,1)S(1)} %merge_chips.1.after.refs_0_.finished), channel_id=1, source_target_pairs={{0,1},{1,2},{2,3},{3,0},{4,5},{5,6},{6,7},{7,4},{8,9},{9,10},{10,1... | collective-permute-start | bytes 49160 | tf_op jit(solution)/shard_map/ppermute | solution.py:333
  24.3 6.7 %collective-permute-start.2 = (bf16[16,4,128]{2,1,0:T(4,128)(2,1)S(1)}, bf16[16,4,128]{2,1,0:T(4,128)(2,1)S(1)}, u32[]{:S(2)}, u32[]{:S(2)}) collective-permute-start(bf16[16,4,128]{2,1,0:T(4,128)(2,1)S(1)} %merge_chips.1.after.refs_0_.finished), channel_id=1, source_target_pairs={{0,2},{1,3},{2,0},{3,1},{4,6},{5,7},{6,4},{7,5},{8,10},{9,11},{10,... | collective-permute-start | bytes 49160 | tf_op jit(solution)/shard_map/ppermute | solution.py:333
  26.9 4.1 %collective-permute-start.1 = (bf16[16,4,128]{2,1,0:T(4,128)(2,1)S(1)}, bf16[16,4,128]{2,1,0:T(4,128)(2,1)S(1)}, u32[]{:S(2)}, u32[]{:S(2)}) collective-permute-start(bf16[16,4,128]{2,1,0:T(4,128)(2,1)S(1)} %merge_chips.1.after.refs_0_.finished), channel_id=1, source_target_pairs={{0,3},{1,0},{2,1},{3,2},{4,7},{5,4},{6,5},{7,6},{8,11},{9,8},{10,9... | collective-permute-start | bytes 49160 | tf_op jit(solution)/shard_map/ppermute | solution.py:333
  31.0 3.3 %collective-permute-start.4 = (bf16[4,16,4,128]{3,2,1,0:T(4,128)(2,1)S(1)}, bf16[4,16,4,128]{3,2,1,0:T(4,128)(2,1)S(1)}, u32[]{:S(2)}, u32[]{:S(2)}) collective-permute-start(bf16[4,16,4,128]{3,2,1,0:T(4,128)(2,1)S(1)} %join_heads.1.mine), channel_id=1, source_target_pairs={{0,4},{4,0},{1,5},{5,1},{2,6},{6,2},{3,7},{7,3},{8,12},{12,8},{9,1... | collective-permute-start | bytes 196616 | tf_op jit(solution)/shard_map/ppermute | solution.py:361
  41.8 15.3 %all-to-all-start.1 = ((f32[128,4,128]{2,1,0:T(4,128)}), f32[128,4,128]{2,1,0:T(4,128)S(1)}, u32[]{:S(2)}, u32[]{:S(2)}) async-start(f32[128,4,128]{2,1,0:T(4,128)} %get-tuple-element.14), calls=%async_computation.1 | async-start | bytes 524288 | tf_op jit(solution)/shard_map/all_to_all | solution.py:387

commit v4 on v3

--- a/solution.py
+++ b/solution.py
@@ -228,7 +228,7 @@
         for half in range(at, at + out_step, CHUNK):
             mixed = jnp.dot(activated, down_w[:, half : half + CHUNK], preferred_element_type=F32)
             for j in range(CHUNK // width):
-                out[half // width + j] = mixed[:, j * width : (j + 1) * width]
+                out[half // width + j] = mixed[:, j * width : (j + 1) * width].astype(BF16)
 
 
 def load_kernel(after, *refs):
@@ -269,7 +269,10 @@
 
 
 def final_kernel(parts, share, out):
-    out[...] = (share[...] + jnp.sum(parts[...], axis=0)).astype(BF16)
+    terms = [parts[i].astype(F32) for i in range(parts.shape[0])]
+    while len(terms) > 1:
+        terms = [terms[i] + terms[i + 1] for i in range(0, len(terms), 2)]
+    out[...] = (share[...] + terms[0]).astype(BF16)
 
 
 VMEM = pl.BlockSpec(memory_space=pltpu.VMEM)
@@ -362,7 +365,7 @@
     mixed, share = pl.pallas_call(
         feed_kernel,
         out_shape=[
-            jax.ShapeDtypeStruct((devices, rows, width), F32),
+            jax.ShapeDtypeStruct((devices, rows, width), BF16),
             jax.ShapeDtypeStruct((rows, width), F32),
         ],
         in_specs=[VMEM] * 5 + [HBM] * 2,

time: 58 us -> 56.6 us (0.976)
  waiting for transfers between devices: 12.3 us -> 11 us
    all_to_all x1, waiting for transfers between devices: 10.4 us -> 9.16 us  [shards(): sums = lax.all_to_all(mixed, ('chip', 'core', 'tp'), 0, 0, tiled=True)]
where the time goes in v4:
time: 56.6 us; the launch traced here: 56.4 us
  blocking collectives  15.8 us (28%)
  Pallas kernels  15.7 us (28%)
  starting transfers between devices  13.2 us (23%)
  waiting for transfers between devices  11 us (19%)
  between operations  0.71 us (1%)
    all_to_all x1, blocking collectives, shards(): blocks = lax.all_to_all(block, 'chip', 0, 0, tiled=True)  15.8 us
    all_to_all x1, waiting for transfers between devices, shards(): sums = lax.all_to_all(mixed, ('chip', 'core', 'tp'), 0, 0, tiled=True)  9.16 us
    pallas_call x1, Pallas kernels, shards(): pl.pallas_call(feed_kernel, out_shape=[jax.ShapeDtypeStruct((devices, row...  7.38 us
    ppermute x3, starting transfers between devices, ring(): lax.ppermute(x, 'tp', [(i, (i - distance) % tp_size) for i in range(tp_si...  5.05 us
    all_to_all x1, starting transfers between devices, shards(): sums = lax.all_to_all(mixed, ('chip', 'core', 'tp'), 0, 0, tiled=True)  4.21 us
    pallas_call x1, Pallas kernels, shards(): pl.pallas_call(attention_kernel, out_shape=[block_f32] * 2, in_specs=[HBM...  3.35 us
    pallas_call x1, Pallas kernels, load(): pl.pallas_call(load_kernel, out_shape=[pltpu.VMEM(x.shape, BF16) for x in...  2.96 us
    ppermute x1, starting transfers between devices, shards(): theirs = lax.ppermute(mine, 'core', swap)  2.42 us
  transfers between devices with their start and end apart: 6, of which 3 were waited for; matrix products, arithmetic and copies ran while one was open for 0% of the time, Pallas kernels for 6%

profile of v4, /device:TPU:1, one launch (start us, length us, event | category | flops | bytes accessed | tf_op | source)
XLA Modules:
  0.0 56.4 jit_solution(4061816522494287686)
XLA Ops:
  0.6 3.3 %attention_partials.1 = (f32[16,8,128]{2,1,0:T(8,128)S(1)}, f32[16,8,128]{2,1,0:T(8,128)S(1)}) custom-call(s32[4]{0:T(128)} %lengths_h.1, s32[4,64]{1,0:T(4,128)} %table_h.1, bf16[4,32,128]{2,1,0:T(8,128)(2,1)} %query_h.1, bf16[8192,128]{1,0:T(8,128)(2,1)} %bitcast.3, bf16[8192,128]{1,0:T(8,128)(2,1)} %bitcast.4), custom_call_target="tpu_custom_call" | custom-call | tf_op jit(solution)/shard_map/attention_partials/pallas_call | solution.py:307
  4.0 1.5 %collective-permute-start = (f32[16,8,128]{2,1,0:T(8,128)S(1)}, f32[16,8,128]{2,1,0:T(8,128)S(1)}, u32[]{:S(2)}, u32[]{:S(2)}) collective-permute-start(f32[16,8,128]{2,1,0:T(8,128)S(1)} %get-tuple-element.10), channel_id=1, source_target_pairs={{0,4},{4,0},{1,5},{5,1},{2,6},{6,2},{3,7},{7,3},{8,12},{12,8},{9,1... | collective-permute-start | bytes 196616 | tf_op jit(solution)/shard_map/ppermute | solution.py:343
  5.5 0.9 %collective-permute-done.received = f32[16,8,128]{2,1,0:T(8,128)S(1)} collective-permute-done((f32[16,8,128]{2,1,0:T(8,128)S(1)}, f32[16,8,128]{2,1,0:T(8,128)S(1)}, u32[]{:S(2)}, u32[]{:S(2)}) %collective-permute-start) | collective-permute-done | bytes 65568 | tf_op jit(solution)/shard_map/ppermute | solution.py:343
  6.4 0.3 merge_cores.1
  6.7 15.8 %all_to_all.10.parts = bf16[16,17,4,128]{3,2,1,0:T(4,128)(2,1)S(1)} all-to-all(bf16[16,17,4,128]{3,2,1,0:T(4,128)(2,1)S(1)} %merge_cores.1), channel_id=1, replica_groups=mesh['chip'=16,'core'=2,'tp'=4] {'chip'}, dimensions={0} | all-to-all | bytes 557056 | tf_op jit(solution)/shard_map/all_to_all | solution.py:345
  22.5 0.5 merge_chips.1.after.refs_0_.finished
  23.0 1.4 %collective-permute-start.3 = (bf16[16,4,128]{2,1,0:T(4,128)(2,1)S(1)}, bf16[16,4,128]{2,1,0:T(4,128)(2,1)S(1)}, u32[]{:S(2)}, u32[]{:S(2)}) collective-permute-start(bf16[16,4,128]{2,1,0:T(4,128)(2,1)S(1)} %merge_chips.1.after.refs_0_.finished), channel_id=1, source_target_pairs={{0,1},{1,2},{2,3},{3,0},{4,5},{5,6},{6,7},{7,4},{8,9},{9,10},{10,1... | collective-permute-start | bytes 49160 | tf_op jit(solution)/shard_map/ppermute | solution.py:336
  24.3 2.6 %collective-permute-start.2 = (bf16[16,4,128]{2,1,0:T(4,128)(2,1)S(1)}, bf16[16,4,128]{2,1,0:T(4,128)(2,1)S(1)}, u32[]{:S(2)}, u32[]{:S(2)}) collective-permute-start(bf16[16,4,128]{2,1,0:T(4,128)(2,1)S(1)} %merge_chips.1.after.refs_0_.finished), channel_id=1, source_target_pairs={{0,2},{1,3},{2,0},{3,1},{4,6},{5,7},{6,4},{7,5},{8,10},{9,11},{10,... | collective-permute-start | bytes 49160 | tf_op jit(solution)/shard_map/ppermute | solution.py:336
  26.9 1.1 %collective-permute-start.1 = (bf16[16,4,128]{2,1,0:T(4,128)(2,1)S(1)}, bf16[16,4,128]{2,1,0:T(4,128)(2,1)S(1)}, u32[]{:S(2)}, u32[]{:S(2)}) collective-permute-start(bf16[16,4,128]{2,1,0:T(4,128)(2,1)S(1)} %merge_chips.1.after.refs_0_.finished), channel_id=1, source_target_pairs={{0,3},{1,0},{2,1},{3,2},{4,7},{5,4},{6,5},{7,6},{8,11},{9,8},{10,9... | collective-permute-start | bytes 49160 | tf_op jit(solution)/shard_map/ppermute | solution.py:336
  28.0 3.0 %load_weights.1 = (bf16[208,16384]{1,0:T(8,128)(2,1)S(1)}, bf16[4,16384]{1,0:T(4,128)(2,1)S(1)}, bf16[128,128]{1,0:T(8,128)(2,1)S(1)}) custom-call(bf16[16,4,128]{2,1,0:T(4,128)(2,1)S(1)} %merge_chips.1.after.refs_0_.finished, bf16[208,16384]{1,0:T(8,128)(2,1)} %refs_0_.1, bf16[4,16384]{1,0:T(4,128)(2,1)} %refs_1_.1, bf16[128,128]{1,0:T(8,128)(2,1)} %bitcast.5), custom_call_target="tpu_custom_call" | custom-call | bytes 6979584 | tf_op jit(solution)/shard_map/load_weights/pallas_call | solution.py:248
  31.0 0.0 collective-permute-done.3.refs_3_
  31.0 0.0 collective-permute-done.2.refs_2_
  31.0 0.0 collective-permute-done.1.refs_1_
  31.0 2.4 %collective-permute-start.4 = (bf16[4,16,4,128]{3,2,1,0:T(4,128)(2,1)S(1)}, bf16[4,16,4,128]{3,2,1,0:T(4,128)(2,1)S(1)}, u32[]{:S(2)}, u32[]{:S(2)}) collective-permute-start(bf16[4,16,4,128]{3,2,1,0:T(4,128)(2,1)S(1)} %join_heads.1.mine), channel_id=1, source_target_pairs={{0,4},{4,0},{1,5},{5,1},{2,6},{6,2},{3,7},{7,3},{8,12},{12,8},{9,1... | collective-permute-start | bytes 196616 | tf_op jit(solution)/shard_map/ppermute | solution.py:364
  33.4 0.9 %collective-permute-done.4.theirs = bf16[4,16,4,128]{3,2,1,0:T(4,128)(2,1)S(1)} collective-permute-done((bf16[4,16,4,128]{3,2,1,0:T(4,128)(2,1)S(1)}, bf16[4,16,4,128]{3,2,1,0:T(4,128)(2,1)S(1)}, u32[]{:S(2)}, u32[]{:S(2)}) %collective-permute-start.4) | collective-permute-done | bytes 65568 | tf_op jit(solution)/shard_map/ppermute | solution.py:364
  34.3 7.4 %feed_forward.1 = (bf16[128,4,128]{2,1,0:T(4,128)(2,1)}, f32[4,128]{1,0:T(4,128)S(1)}) custom-call(bf16[4,16,4,128]{3,2,1,0:T(4,128)(2,1)S(1)} %join_heads.1.mine, bf16[4,16,4,128]{3,2,1,0:T(4,128)(2,1)S(1)} %collective-permute-done.4.theirs, bf16[4,16384]{1,0:T(4,128)(2,1)S(1)} %get-tuple-element.12.residual, ...), custom_call_target="tpu_custom_call" | custom-call | tf_op jit(solution)/shard_map/feed_forward/pallas_call | solution.py:365
  41.7 4.2 %all-to-all-start.1 = ((bf16[128,4,128]{2,1,0:T(4,128)(2,1)}), bf16[128,4,128]{2,1,0:T(4,128)(2,1)S(1)}, u32[]{:S(2)}, u32[]{:S(2)}) async-start(bf16[128,4,128]{2,1,0:T(4,128)(2,1)} %get-tuple-element.14), calls=%async_computation.1 | async-start | bytes 262144 | tf_op jit(solution)/shard_map/all_to_all | solution.py:390
  45.9 0.7 %own_heads.1 = bf16[4,32,128]{2,1,0:T(8,128)(2,1)} custom-call(bf16[16,4,128]{2,1,0:T(4,128)(2,1)S(1)} %merge_chips.1.after.refs_0_.finished, bf16[4,16,4,128]{3,2,1,0:T(4,128)(2,1)S(1)} %collective-permute-done.4.theirs, f32[4,128]{1,0:T(4,128)S(1)} %get-tuple-element.15.share), custom_call_target="tpu_custom_call" | custom-call | tf_op jit(solution)/shard_map/own_heads/pallas_call | solution.py:325
  46.6 9.2 %all-to-all-done.1.parts = bf16[128,4,128]{2,1,0:T(4,128)(2,1)S(1)} async-done(((bf16[128,4,128]{2,1,0:T(4,128)(2,1)}), bf16[128,4,128]{2,1,0:T(4,128)(2,1)S(1)}, u32[]{:S(2)}, u32[]{:S(2)}) %all-to-all-start.1) | async-done | bytes 131104 | tf_op jit(solution)/shard_map/all_to_all | solution.py:390
  55.8 0.6 %add_shares.1 = bf16[4,128]{1,0:T(4,128)(2,1)} custom-call(bf16[128,4,128]{2,1,0:T(4,128)(2,1)S(1)} %all-to-all-done.1.parts, f32[4,128]{1,0:T(4,128)S(1)} %get-tuple-element.15.share), custom_call_target="tpu_custom_call" | custom-call | tf_op jit(solution)/shard_map/add_shares/pallas_call | solution.py:325
  (1 shorter events, 0.0 us)
Async XLA Ops:
  4.0 2.4 %collective-permute-start = (f32[16,8,128]{2,1,0:T(8,128)S(1)}, f32[16,8,128]{2,1,0:T(8,128)S(1)}, u32[]{:S(2)}, u32[]{:S(2)}) collective-permute-start(f32[16,8,128]{2,1,0:T(8,128)S(1)} %get-tuple-element.10), channel_id=1, source_target_pairs={{0,4},{4,0},{1,5},{5,1},{2,6},{6,2},{3,7},{7,3},{8,12},{12,8},{9,1... | collective-permute-start | bytes 196616 | tf_op jit(solution)/shard_map/ppermute | solution.py:343
  23.0 8.0 %collective-permute-start.3 = (bf16[16,4,128]{2,1,0:T(4,128)(2,1)S(1)}, bf16[16,4,128]{2,1,0:T(4,128)(2,1)S(1)}, u32[]{:S(2)}, u32[]{:S(2)}) collective-permute-start(bf16[16,4,128]{2,1,0:T(4,128)(2,1)S(1)} %merge_chips.1.after.refs_0_.finished), channel_id=1, source_target_pairs={{0,1},{1,2},{2,3},{3,0},{4,5},{5,6},{6,7},{7,4},{8,9},{9,10},{10,1... | collective-permute-start | bytes 49160 | tf_op jit(solution)/shard_map/ppermute | solution.py:336
  24.3 6.7 %collective-permute-start.2 = (bf16[16,4,128]{2,1,0:T(4,128)(2,1)S(1)}, bf16[16,4,128]{2,1,0:T(4,128)(2,1)S(1)}, u32[]{:S(2)}, u32[]{:S(2)}) collective-permute-start(bf16[16,4,128]{2,1,0:T(4,128)(2,1)S(1)} %merge_chips.1.after.refs_0_.finished), channel_id=1, source_target_pairs={{0,2},{1,3},{2,0},{3,1},{4,6},{5,7},{6,4},{7,5},{8,10},{9,11},{10,... | collective-permute-start | bytes 49160 | tf_op jit(solution)/shard_map/ppermute | solution.py:336
  26.9 4.1 %collective-permute-start.1 = (bf16[16,4,128]{2,1,0:T(4,128)(2,1)S(1)}, bf16[16,4,128]{2,1,0:T(4,128)(2,1)S(1)}, u32[]{:S(2)}, u32[]{:S(2)}) collective-permute-start(bf16[16,4,128]{2,1,0:T(4,128)(2,1)S(1)} %merge_chips.1.after.refs_0_.finished), channel_id=1, source_target_pairs={{0,3},{1,0},{2,1},{3,2},{4,7},{5,4},{6,5},{7,6},{8,11},{9,8},{10,9... | collective-permute-start | bytes 49160 | tf_op jit(solution)/shard_map/ppermute | solution.py:336
  31.0 3.3 %collective-permute-start.4 = (bf16[4,16,4,128]{3,2,1,0:T(4,128)(2,1)S(1)}, bf16[4,16,4,128]{3,2,1,0:T(4,128)(2,1)S(1)}, u32[]{:S(2)}, u32[]{:S(2)}) collective-permute-start(bf16[4,16,4,128]{3,2,1,0:T(4,128)(2,1)S(1)} %join_heads.1.mine), channel_id=1, source_target_pairs={{0,4},{4,0},{1,5},{5,1},{2,6},{6,2},{3,7},{7,3},{8,12},{12,8},{9,1... | collective-permute-start | bytes 196616 | tf_op jit(solution)/shard_map/ppermute | solution.py:364
  41.7 14.1 %all-to-all-start.1 = ((bf16[128,4,128]{2,1,0:T(4,128)(2,1)}), bf16[128,4,128]{2,1,0:T(4,128)(2,1)S(1)}, u32[]{:S(2)}, u32[]{:S(2)}) async-start(bf16[128,4,128]{2,1,0:T(4,128)(2,1)} %get-tuple-element.14), calls=%async_computation.1 | async-start | bytes 262144 | tf_op jit(solution)/shard_map/all_to_all | solution.py:390

commit v5 on v4

--- a/solution.py
+++ b/solution.py
@@ -14,7 +14,7 @@
 MIB = 1 << 20
 NT = (((1,), (1,)), ((), ()))
 PAGES_PER_DOT = 8
-PARTS = 4
+PARTS = 8
 CHUNK = 2048
 IN_STEPS = 8
 OUT_STEPS = 4
@@ -200,7 +200,8 @@
     squares = jnp.zeros((rows, width), F32)
     for part, core in ((mine, kv % 2), (theirs, 1 - kv % 2)):
         for distance in range(groups):
-            base = ((tp + distance) % groups) * (2 * half) + core * half
+            held = core if distance == 0 else 1 - core
+            base = ((tp + distance) % groups) * (2 * half) + held * half
             for i in range(half):
                 cols = pl.ds(pl.multiple_of((base + i) * width, width), width)
                 value = residual[:, cols].astype(F32) + part[distance, i].astype(F32)
@@ -257,22 +258,19 @@
     )(after, *in_hbm(*arrays))
 
 
-def own_heads_kernel(finished, theirs, share, out):
+def final_kernel(parts, share, finished, theirs, layer_out, attention):
     half, rows, width = finished.shape
     first = lax.axis_index("core") == 0
     mine, other = finished[...].astype(F32), theirs[0].astype(F32)
     low = jnp.where(first, mine, other)
     high = jnp.where(first, other, mine)
     for row in range(rows):
-        out[row, :half] = low[:, row, :].astype(BF16)
-        out[row, half:] = high[:, row, :].astype(BF16)
-
-
-def final_kernel(parts, share, out):
+        attention[row, :half] = low[:, row, :].astype(BF16)
+        attention[row, half:] = high[:, row, :].astype(BF16)
     terms = [parts[i].astype(F32) for i in range(parts.shape[0])]
     while len(terms) > 1:
         terms = [terms[i] + terms[i + 1] for i in range(0, len(terms), 2)]
-    out[...] = (share[...] + terms[0]).astype(BF16)
+    layer_out[...] = (share[...] + terms[0]).astype(BF16)
 
 
 VMEM = pl.BlockSpec(memory_space=pltpu.VMEM)
@@ -326,14 +324,22 @@
             kernel,
             out_shape=out_shape,
             in_specs=[VMEM] * len(operands),
-            out_specs=VMEM,
+            out_specs=jax.tree.map(lambda _: VMEM, out_shape),
             compiler_params=small,
             name=name,
         )(*operands)
 
     def ring(x):
         one, three, two = (
-            lax.ppermute(x, "tp", [(i, (i - distance) % tp_size) for i in range(tp_size)])
+            lax.ppermute(
+                x,
+                ("core", "tp"),
+                [
+                    (core * tp_size + i, (1 - core) * tp_size + (i - distance) % tp_size)
+                    for core in range(2)
+                    for i in range(tp_size)
+                ],
+            )
             for distance in (1, 3, 2)
         )
         return one, two, three
@@ -388,18 +394,15 @@
         *in_hbm(up_weight, down_weight),
     )
     sums = lax.all_to_all(mixed, ("chip", "core", "tp"), 0, 0, tiled=True)
-    layer_out = call(
-        final_kernel, jax.ShapeDtypeStruct((rows, width), BF16), "add_shares", sums, share
-    )
-    attention = call(
-        own_heads_kernel,
-        jax.ShapeDtypeStruct(query.shape, BF16),
-        "own_heads",
+    return call(
+        final_kernel,
+        [jax.ShapeDtypeStruct((rows, width), BF16), jax.ShapeDtypeStruct(query.shape, BF16)],
+        "add_shares",
+        sums,
+        share,
         finished,
         theirs,
-        share,
-    )
-    return layer_out, attention
+    )
 
 
 def solution(mesh):

time: 56.6 us -> 55.4 us (0.979)
  blocking collectives: 15.8 us -> 29.5 us
  waiting for transfers between devices: 11 us -> 2.15 us
  starting transfers between devices: 13.2 us -> 8.31 us
  Pallas kernels: 15.7 us -> 14.5 us
    all_to_all x0 -> x1, blocking collectives: none -> 13.8 us  [shards(): sums = lax.all_to_all(mixed, ('chip', 'core', 'tp'), 0, 0, tiled=True)]
    all_to_all x1 -> x0, waiting for transfers between devices: 9.16 us -> none  [shards(): sums = lax.all_to_all(mixed, ('chip', 'core', 'tp'), 0, 0, tiled=True)]
    all_to_all x1 -> x0, starting transfers between devices: 4.21 us -> none  [shards(): sums = lax.all_to_all(mixed, ('chip', 'core', 'tp'), 0, 0, tiled=True)]
    ppermute x1, starting transfers between devices: 2.42 us -> 0.09 us  [shards(): theirs = lax.ppermute(mine, 'core', swap)]
    ppermute x3, starting transfers between devices: 5.05 us -> 6.73 us  [ring(): lax.ppermute(x, ('core', 'tp'), [(core * tp_size + i, (1 - core) * tp_siz...]
    pallas_call x1, Pallas kernels: 7.38 us -> 6.73 us  [shards(): pl.pallas_call(feed_kernel, out_shape=[jax.ShapeDtypeStruct((devices, row...]
    pallas_call x5 -> x4, Pallas kernels: 2.06 us -> 1.45 us  [call(): pl.pallas_call(kernel, out_shape=out_shape, in_specs=[VMEM] * len(operand...]
  transfers between devices with their start and end apart: 6 -> 5, of which waited for: 3 -> 2; matrix products, arithmetic and copies ran while one was open for 0% -> 0% of each run, Pallas kernels for 6% -> 5%
where the time goes in v5:
time: 55.4 us; the launch traced here: 55.3 us
  blocking collectives  29.5 us (53%)
  Pallas kernels  14.5 us (26%)
  starting transfers between devices  8.31 us (15%)
  waiting for transfers between devices  2.15 us (4%)
  between operations  0.71 us (1%)
    all_to_all x1, blocking collectives, shards(): blocks = lax.all_to_all(block, 'chip', 0, 0, tiled=True)  15.8 us
    all_to_all x1, blocking collectives, shards(): sums = lax.all_to_all(mixed, ('chip', 'core', 'tp'), 0, 0, tiled=True)  13.8 us
    pallas_call x1, Pallas kernels, shards(): pl.pallas_call(feed_kernel, out_shape=[jax.ShapeDtypeStruct((devices, row...  6.73 us
    ppermute x3, starting transfers between devices, ring(): lax.ppermute(x, ('core', 'tp'), [(core * tp_size + i, (1 - core) * tp_siz...  6.73 us
    pallas_call x1, Pallas kernels, shards(): pl.pallas_call(attention_kernel, out_shape=[block_f32] * 2, in_specs=[HBM...  3.4 us
    pallas_call x1, Pallas kernels, load(): pl.pallas_call(load_kernel, out_shape=[pltpu.VMEM(x.shape, BF16) for x in...  2.96 us
    ppermute x1, starting transfers between devices, shards(): lax.ppermute(send, 'core', swap)  1.5 us
    pallas_call x4, Pallas kernels, call(): pl.pallas_call(kernel, out_shape=out_shape, in_specs=[VMEM] * len(operand...  1.45 us
  transfers between devices with their start and end apart: 5, of which 2 were waited for; matrix products, arithmetic and copies ran while one was open for 0% of the time, Pallas kernels for 5%

profile of v5, /device:TPU:1, one launch (start us, length us, event | category | flops | bytes accessed | tf_op | source)
XLA Modules:
  0.0 55.3 jit_solution(4230487995615409785)
XLA Ops:
  0.6 3.4 %attention_partials.1 = (f32[16,8,128]{2,1,0:T(8,128)S(1)}, f32[16,8,128]{2,1,0:T(8,128)S(1)}) custom-call(s32[4]{0:T(128)} %lengths_h.1, s32[4,64]{1,0:T(4,128)} %table_h.1, bf16[4,32,128]{2,1,0:T(8,128)(2,1)} %query_h.1, bf16[8192,128]{1,0:T(8,128)(2,1)} %bitcast.3, bf16[8192,128]{1,0:T(8,128)(2,1)} %bitcast.4), custom_call_target="tpu_custom_call" | custom-call | tf_op jit(solution)/shard_map/attention_partials/pallas_call | solution.py:305
  4.0 1.5 %collective-permute-start = (f32[16,8,128]{2,1,0:T(8,128)S(1)}, f32[16,8,128]{2,1,0:T(8,128)S(1)}, u32[]{:S(2)}, u32[]{:S(2)}) collective-permute-start(f32[16,8,128]{2,1,0:T(8,128)S(1)} %get-tuple-element.10), channel_id=1, source_target_pairs={{0,4},{4,0},{1,5},{5,1},{2,6},{6,2},{3,7},{7,3},{8,12},{12,8},{9,1... | collective-permute-start | bytes 196616 | tf_op jit(solution)/shard_map/ppermute | solution.py:349
  5.5 0.9 %collective-permute-done.received = f32[16,8,128]{2,1,0:T(8,128)S(1)} collective-permute-done((f32[16,8,128]{2,1,0:T(8,128)S(1)}, f32[16,8,128]{2,1,0:T(8,128)S(1)}, u32[]{:S(2)}, u32[]{:S(2)}) %collective-permute-start) | collective-permute-done | bytes 65568 | tf_op jit(solution)/shard_map/ppermute | solution.py:349
  6.4 0.3 merge_cores.1
  6.7 15.8 %all_to_all.10.parts = bf16[16,17,4,128]{3,2,1,0:T(4,128)(2,1)S(1)} all-to-all(bf16[16,17,4,128]{3,2,1,0:T(4,128)(2,1)S(1)} %merge_cores.1), channel_id=1, replica_groups=mesh['chip'=16,'core'=2,'tp'=4] {'chip'}, dimensions={0} | all-to-all | bytes 557056 | tf_op jit(solution)/shard_map/all_to_all | solution.py:351
  22.5 0.5 merge_chips.1.after.refs_0_.finished
  23.0 2.8 %collective-permute-start.3 = (bf16[16,4,128]{2,1,0:T(4,128)(2,1)S(1)}, bf16[16,4,128]{2,1,0:T(4,128)(2,1)S(1)}, u32[]{:S(2)}, u32[]{:S(2)}) collective-permute-start(bf16[16,4,128]{2,1,0:T(4,128)(2,1)S(1)} %merge_chips.1.after.refs_0_.finished), channel_id=1, source_target_pairs={{0,5},{1,6},{2,7},{3,4},{4,1},{5,2},{6,3},{7,0},{8,13},{9,14},{10,... | collective-permute-start | bytes 49160 | tf_op jit(solution)/shard_map/ppermute | solution.py:334
  25.8 1.7 %collective-permute-start.2 = (bf16[16,4,128]{2,1,0:T(4,128)(2,1)S(1)}, bf16[16,4,128]{2,1,0:T(4,128)(2,1)S(1)}, u32[]{:S(2)}, u32[]{:S(2)}) collective-permute-start(bf16[16,4,128]{2,1,0:T(4,128)(2,1)S(1)} %merge_chips.1.after.refs_0_.finished), channel_id=1, source_target_pairs={{0,6},{1,7},{2,4},{3,5},{4,2},{5,3},{6,0},{7,1},{8,14},{9,15},{10,... | collective-permute-start | bytes 49160 | tf_op jit(solution)/shard_map/ppermute | solution.py:334
  27.5 2.3 %collective-permute-start.1 = (bf16[16,4,128]{2,1,0:T(4,128)(2,1)S(1)}, bf16[16,4,128]{2,1,0:T(4,128)(2,1)S(1)}, u32[]{:S(2)}, u32[]{:S(2)}) collective-permute-start(bf16[16,4,128]{2,1,0:T(4,128)(2,1)S(1)} %merge_chips.1.after.refs_0_.finished), channel_id=1, source_target_pairs={{0,7},{1,4},{2,5},{3,6},{4,3},{5,0},{6,1},{7,2},{8,15},{9,12},{10,... | collective-permute-start | bytes 49160 | tf_op jit(solution)/shard_map/ppermute | solution.py:334
  29.7 3.0 %load_weights.1 = (bf16[208,16384]{1,0:T(8,128)(2,1)S(1)}, bf16[4,16384]{1,0:T(4,128)(2,1)S(1)}, bf16[128,128]{1,0:T(8,128)(2,1)S(1)}) custom-call(bf16[16,4,128]{2,1,0:T(4,128)(2,1)S(1)} %merge_chips.1.after.refs_0_.finished, bf16[208,16384]{1,0:T(8,128)(2,1)} %refs_0_.1, bf16[4,16384]{1,0:T(4,128)(2,1)} %refs_1_.1, bf16[128,128]{1,0:T(8,128)(2,1)} %bitcast.5), custom_call_target="tpu_custom_call" | custom-call | bytes 6979584 | tf_op jit(solution)/shard_map/load_weights/pallas_call | solution.py:249
  32.7 0.0 collective-permute-done.3.refs_3_
  32.7 0.0 collective-permute-done.2.refs_2_
  32.7 0.0 collective-permute-done.1.refs_1_
  32.7 0.1 collective-permute-start.4
  32.8 1.2 %collective-permute-done.4.theirs = bf16[4,16,4,128]{3,2,1,0:T(4,128)(2,1)S(1)} collective-permute-done((bf16[4,16,4,128]{3,2,1,0:T(4,128)(2,1)S(1)}, bf16[4,16,4,128]{3,2,1,0:T(4,128)(2,1)S(1)}, u32[]{:S(2)}, u32[]{:S(2)}) %collective-permute-start.4) | collective-permute-done | bytes 65568 | tf_op jit(solution)/shard_map/ppermute | solution.py:370
  34.1 6.7 %feed_forward.1 = (bf16[128,4,128]{2,1,0:T(4,128)(2,1)S(1)}, f32[4,128]{1,0:T(4,128)S(1)}) custom-call(bf16[4,16,4,128]{3,2,1,0:T(4,128)(2,1)S(1)} %join_heads.1.mine, bf16[4,16,4,128]{3,2,1,0:T(4,128)(2,1)S(1)} %collective-permute-done.4.theirs, bf16[4,16384]{1,0:T(4,128)(2,1)S(1)} %get-tuple-element.12.residual, ...), custom_call_target="tpu_custom_call" | custom-call | tf_op jit(solution)/shard_map/feed_forward/pallas_call | solution.py:371
  40.8 13.8 %all_to_all.11.parts = bf16[128,4,128]{2,1,0:T(4,128)(2,1)S(1)} all-to-all(bf16[128,4,128]{2,1,0:T(4,128)(2,1)S(1)} %get-tuple-element.14), channel_id=1, replica_groups=mesh['chip'=16,'core'=2,'tp'=4] {'chip','core','tp'}, dimensions={0} | all-to-all | bytes 262144 | tf_op jit(solution)/shard_map/all_to_all | solution.py:396
  54.6 0.7 %add_shares.1 = (bf16[4,128]{1,0:T(4,128)(2,1)}, bf16[4,32,128]{2,1,0:T(8,128)(2,1)}) custom-call(bf16[128,4,128]{2,1,0:T(4,128)(2,1)S(1)} %all_to_all.11.parts, f32[4,128]{1,0:T(4,128)S(1)} %get-tuple-element.15.share, bf16[16,4,128]{2,1,0:T(4,128)(2,1)S(1)} %merge_chips.1.after.refs_0_.finished, bf16[4,16,4,128]{3,2,1,0:T(4,128)(2,1)S(1)} %collective-permute-done.4.theirs), custom_call_target="tpu_custom_call" | custom-call | tf_op jit(solution)/shard_map/add_shares/pallas_call | solution.py:323
  (1 shorter events, 0.0 us)
Async XLA Ops:
  4.0 2.4 %collective-permute-start = (f32[16,8,128]{2,1,0:T(8,128)S(1)}, f32[16,8,128]{2,1,0:T(8,128)S(1)}, u32[]{:S(2)}, u32[]{:S(2)}) collective-permute-start(f32[16,8,128]{2,1,0:T(8,128)S(1)} %get-tuple-element.10), channel_id=1, source_target_pairs={{0,4},{4,0},{1,5},{5,1},{2,6},{6,2},{3,7},{7,3},{8,12},{12,8},{9,1... | collective-permute-start | bytes 196616 | tf_op jit(solution)/shard_map/ppermute | solution.py:349
  23.0 9.7 %collective-permute-start.3 = (bf16[16,4,128]{2,1,0:T(4,128)(2,1)S(1)}, bf16[16,4,128]{2,1,0:T(4,128)(2,1)S(1)}, u32[]{:S(2)}, u32[]{:S(2)}) collective-permute-start(bf16[16,4,128]{2,1,0:T(4,128)(2,1)S(1)} %merge_chips.1.after.refs_0_.finished), channel_id=1, source_target_pairs={{0,5},{1,6},{2,7},{3,4},{4,1},{5,2},{6,3},{7,0},{8,13},{9,14},{10,... | collective-permute-start | bytes 49160 | tf_op jit(solution)/shard_map/ppermute | solution.py:334
  25.8 7.0 %collective-permute-start.2 = (bf16[16,4,128]{2,1,0:T(4,128)(2,1)S(1)}, bf16[16,4,128]{2,1,0:T(4,128)(2,1)S(1)}, u32[]{:S(2)}, u32[]{:S(2)}) collective-permute-start(bf16[16,4,128]{2,1,0:T(4,128)(2,1)S(1)} %merge_chips.1.after.refs_0_.finished), channel_id=1, source_target_pairs={{0,6},{1,7},{2,4},{3,5},{4,2},{5,3},{6,0},{7,1},{8,14},{9,15},{10,... | collective-permute-start | bytes 49160 | tf_op jit(solution)/shard_map/ppermute | solution.py:334
  27.5 5.3 %collective-permute-start.1 = (bf16[16,4,128]{2,1,0:T(4,128)(2,1)S(1)}, bf16[16,4,128]{2,1,0:T(4,128)(2,1)S(1)}, u32[]{:S(2)}, u32[]{:S(2)}) collective-permute-start(bf16[16,4,128]{2,1,0:T(4,128)(2,1)S(1)} %merge_chips.1.after.refs_0_.finished), channel_id=1, source_target_pairs={{0,7},{1,4},{2,5},{3,6},{4,3},{5,0},{6,1},{7,2},{8,15},{9,12},{10,... | collective-permute-start | bytes 49160 | tf_op jit(solution)/shard_map/ppermute | solution.py:334
  32.7 1.3 %collective-permute-start.4 = (bf16[4,16,4,128]{3,2,1,0:T(4,128)(2,1)S(1)}, bf16[4,16,4,128]{3,2,1,0:T(4,128)(2,1)S(1)}, u32[]{:S(2)}, u32[]{:S(2)}) collective-permute-start(bf16[4,16,4,128]{3,2,1,0:T(4,128)(2,1)S(1)} %join_heads.1.mine), channel_id=1, source_target_pairs={{0,4},{4,0},{1,5},{5,1},{2,6},{6,2},{3,7},{7,3},{8,12},{12,8},{9,1... | collective-permute-start | bytes 196616 | tf_op jit(solution)/shard_map/ppermute | solution.py:370

commit v6 on v5

--- a/solution.py
+++ b/solution.py
@@ -18,6 +18,7 @@
 CHUNK = 2048
 IN_STEPS = 8
 OUT_STEPS = 4
+UP_HELD = 2
 
 
 def kv_index():
@@ -115,7 +116,7 @@
         out[i, heads] = terms
 
 
-def merge_cores_kernel(keep, received, out):
+def merge_cores_kernel(keep, received, loaded, out):
     heads, double, width = keep.shape
     rows = double // 2
     mine, theirs = keep[...], received[...]
@@ -166,6 +167,7 @@
     residual,
     gain,
     gate_w,
+    up_first,
     up_h,
     down_h,
     out,
@@ -183,18 +185,18 @@
     in_step = features // IN_STEPS
     out_step = features // OUT_STEPS
 
-    def pieces(source, target, which, steps):
+    def pieces(source, target, which, first, steps):
         step = features // steps
         copies = []
-        for i in range(steps):
+        for i in range(first, steps):
             at = pl.ds(i * step, step)
             copies.append(
                 pltpu.make_async_copy(source.at[:, at], target.at[:, at], sems.at[which, i])
             )
         return copies
 
-    up_copies = pieces(up_h, up_w, 0, IN_STEPS)
-    down_copies = pieces(down_h, down_w, 1, OUT_STEPS)
+    up_copies = pieces(up_h, up_w, 0, UP_HELD, IN_STEPS)
+    down_copies = pieces(down_h, down_w, 1, 0, OUT_STEPS)
     for copy in up_copies + down_copies:
         copy.start()
     squares = jnp.zeros((rows, width), F32)
@@ -219,9 +221,11 @@
     for i in range(IN_STEPS):
         at = i * in_step
         x = normed[:, at : at + in_step]
-        up_copies[i].wait()
+        if i >= UP_HELD:
+            up_copies[i - UP_HELD].wait()
+        up_block = (up_first if i < UP_HELD else up_w)[:, at : at + in_step]
         gate += lax.dot_general(x, gate_w[:, at : at + in_step], NT, preferred_element_type=F32)
-        up += lax.dot_general(x, up_w[:, at : at + in_step], NT, preferred_element_type=F32)
+        up += lax.dot_general(x, up_block, NT, preferred_element_type=F32)
     activated = (gate / (1.0 + jnp.exp(-gate)) * up).astype(BF16)
     for i in range(OUT_STEPS):
         at = i * out_step
@@ -232,26 +236,30 @@
                 out[half // width + j] = mixed[:, j * width : (j + 1) * width].astype(BF16)
 
 
-def load_kernel(after, *refs):
-    count = len(refs) // 2
+def load_kernel(ranges, after, *refs):
+    count = len(ranges)
     sems = refs[2 * count]
     copies = []
-    for i in range(count):
-        copies.append(pltpu.make_async_copy(refs[i], refs[count + i], sems.at[i]))
+    for i, (first, last) in enumerate(ranges):
+        source = refs[i].at[:, pl.ds(first, last - first)]
+        copies.append(pltpu.make_async_copy(source, refs[count + i], sems.at[i]))
     for copy in copies:
         copy.start()
     for copy in copies:
         copy.wait()
 
 
-def load(after, *arrays):
-    moved = sum(2 * x.size for x in arrays)
+def load(after, *parts):
+    arrays = [array for array, _, _ in parts]
+    ranges = [(first, last) for _, first, last in parts]
+    shapes = [(array.shape[0], last - first) for array, first, last in parts]
+    moved = sum(2 * shape[0] * shape[1] for shape in shapes)
     return pl.pallas_call(
-        load_kernel,
-        out_shape=[pltpu.VMEM(x.shape, BF16) for x in arrays],
-        in_specs=[VMEM] + [HBM] * len(arrays),
-        out_specs=[VMEM] * len(arrays),
-        scratch_shapes=[pltpu.SemaphoreType.DMA((len(arrays),))],
+        functools.partial(load_kernel, ranges),
+        out_shape=[pltpu.VMEM(shape, BF16) for shape in shapes],
+        in_specs=[VMEM] + [HBM] * len(parts),
+        out_specs=[VMEM] * len(parts),
+        scratch_shapes=[pltpu.SemaphoreType.DMA((len(parts),))],
         compiler_params=pltpu.CompilerParams(vmem_limit_bytes=16 * MIB),
         cost_estimate=pl.CostEstimate(flops=0, bytes_accessed=moved, transcendentals=0),
         name="load_weights",
@@ -345,9 +353,10 @@
         return one, two, three
 
     swap = [(0, 1), (1, 0)]
-    block = call(
-        merge_cores_kernel, packed, "merge_cores", keep, lax.ppermute(send, "core", swap)
-    )
+    received = lax.ppermute(send, "core", swap)
+    features = residual.shape[1]
+    (up_first,) = load(keep, (up_weight, 0, UP_HELD * (features // IN_STEPS)))
+    block = call(merge_cores_kernel, packed, "merge_cores", keep, received, up_first)
     blocks = lax.all_to_all(block, "chip", 0, 0, tiled=True)
     finished = call(
         merge_chips_kernel,
@@ -356,8 +365,9 @@
         blocks,
     )
     around = ring(finished)
+    gains = norm_gain.reshape(devices, width)
     gate, res, gain = load(
-        finished, gate_weight, residual, norm_gain.reshape(devices, width)
+        finished, (gate_weight, 0, features), (residual, 0, features), (gains, 0, width)
     )
     mine = call(
         join_kernel,
@@ -374,7 +384,7 @@
             jax.ShapeDtypeStruct((devices, rows, width), BF16),
             jax.ShapeDtypeStruct((rows, width), F32),
         ],
-        in_specs=[VMEM] * 5 + [HBM] * 2,
+        in_specs=[VMEM] * 6 + [HBM] * 2,
         out_specs=[VMEM] * 2,
         scratch_shapes=[
             pltpu.VMEM(up_weight.shape, BF16),
@@ -391,6 +401,7 @@
         res,
         gain,
         gate,
+        up_first,
         *in_hbm(up_weight, down_weight),
     )
     sums = lax.all_to_all(mixed, ("chip", "core", "tp"), 0, 0, tiled=True)

time: 55.4 us -> 55.1 us (level)
  waiting for transfers between devices: 2.15 us -> 1.25 us
    pallas_call x1 -> x2, Pallas kernels: 2.96 us -> 4.42 us  [load(): pl.pallas_call(functools.partial(load_kernel, ranges), out_shape=[pltpu.V...]
    pallas_call x1, Pallas kernels: 6.73 us -> 5.77 us  [shards(): pl.pallas_call(feed_kernel, out_shape=[jax.ShapeDtypeStruct((devices, row...]
    ppermute x1, waiting for transfers between devices: 0.9 us -> 0.01 us  [shards(): received = lax.ppermute(send, 'core', swap)]
  transfers between devices with their start and end apart: 5 -> 5, of which waited for: 2 -> 1; matrix products, arithmetic and copies ran while one was open for 0% -> 0% of each run, Pallas kernels for 5% -> 8%
where the time goes in v6:
time: 55.1 us; the launch traced here: 54.9 us
  blocking collectives  29.9 us (54%)
  Pallas kernels  15 us (27%)
  starting transfers between devices  7.95 us (14%)
  waiting for transfers between devices  1.25 us (2%)
  between operations  0.73 us (1%)
    all_to_all x1, blocking collectives, shards(): blocks = lax.all_to_all(block, 'chip', 0, 0, tiled=True)  16.2 us
    all_to_all x1, blocking collectives, shards(): sums = lax.all_to_all(mixed, ('chip', 'core', 'tp'), 0, 0, tiled=True)  13.8 us
    ppermute x3, starting transfers between devices, ring(): lax.ppermute(x, ('core', 'tp'), [(core * tp_size + i, (1 - core) * tp_siz...  6.36 us
    pallas_call x1, Pallas kernels, shards(): pl.pallas_call(feed_kernel, out_shape=[jax.ShapeDtypeStruct((devices, row...  5.77 us
    pallas_call x2, Pallas kernels, load(): pl.pallas_call(functools.partial(load_kernel, ranges), out_shape=[pltpu.V...  4.42 us
    pallas_call x1, Pallas kernels, shards(): pl.pallas_call(attention_kernel, out_shape=[block_f32] * 2, in_specs=[HBM...  3.4 us
    ppermute x1, starting transfers between devices, shards(): received = lax.ppermute(send, 'core', swap)  1.5 us
    pallas_call x4, Pallas kernels, call(): pl.pallas_call(kernel, out_shape=out_shape, in_specs=[VMEM] * len(operand...  1.45 us
  transfers between devices with their start and end apart: 5, of which 1 were waited for; matrix products, arithmetic and copies ran while one was open for 0% of the time, Pallas kernels for 8%

profile of v6, /device:TPU:1, one launch (start us, length us, event | category | flops | bytes accessed | tf_op | source)
XLA Modules:
  0.0 54.9 jit_solution(12416070904562134355)
XLA Ops:
  0.6 3.4 %attention_partials.1 = (f32[16,8,128]{2,1,0:T(8,128)S(1)}, f32[16,8,128]{2,1,0:T(8,128)S(1)}) custom-call(s32[4]{0:T(128)} %lengths_h.1, s32[4,64]{1,0:T(4,128)} %table_h.1, bf16[4,32,128]{2,1,0:T(8,128)(2,1)} %query_h.1, bf16[8192,128]{1,0:T(8,128)(2,1)} %bitcast.3, bf16[8192,128]{1,0:T(8,128)(2,1)} %bitcast.4), custom_call_target="tpu_custom_call" | custom-call | tf_op jit(solution)/shard_map/attention_partials/pallas_call | solution.py:313
  4.0 1.5 %collective-permute-start = (f32[16,8,128]{2,1,0:T(8,128)S(1)}, f32[16,8,128]{2,1,0:T(8,128)S(1)}, u32[]{:S(2)}, u32[]{:S(2)}) collective-permute-start(f32[16,8,128]{2,1,0:T(8,128)S(1)} %get-tuple-element.10), channel_id=1, source_target_pairs={{0,4},{4,0},{1,5},{5,1},{2,6},{6,2},{3,7},{7,3},{8,12},{12,8},{9,1... | collective-permute-start | bytes 196616 | tf_op jit(solution)/shard_map/ppermute | solution.py:356
  5.5 1.5 %load_weights.2.loaded.up_first = bf16[208,4096]{1,0:T(8,128)(2,1)S(1)} custom-call(f32[16,8,128]{2,1,0:T(8,128)S(1)} %get-tuple-element.9.after.keep, bf16[208,16384]{1,0:T(8,128)(2,1)} %up_h.1), custom_call_target="tpu_custom_call" | custom-call | bytes 1703936 | tf_op jit(solution)/shard_map/load_weights/pallas_call | solution.py:257
  7.0 0.0 collective-permute-done.received
  7.0 0.3 merge_cores.1
  7.3 16.2 %all_to_all.10.parts = bf16[16,17,4,128]{3,2,1,0:T(4,128)(2,1)S(1)} all-to-all(bf16[16,17,4,128]{3,2,1,0:T(4,128)(2,1)S(1)} %merge_cores.1), channel_id=1, replica_groups=mesh['chip'=16,'core'=2,'tp'=4] {'chip'}, dimensions={0} | all-to-all | bytes 557056 | tf_op jit(solution)/shard_map/all_to_all | solution.py:360
  23.4 0.5 merge_chips.1.after.refs_0_.finished
  23.9 2.4 %collective-permute-start.3 = (bf16[16,4,128]{2,1,0:T(4,128)(2,1)S(1)}, bf16[16,4,128]{2,1,0:T(4,128)(2,1)S(1)}, u32[]{:S(2)}, u32[]{:S(2)}) collective-permute-start(bf16[16,4,128]{2,1,0:T(4,128)(2,1)S(1)} %merge_chips.1.after.refs_0_.finished), channel_id=1, source_target_pairs={{0,5},{1,6},{2,7},{3,4},{4,1},{5,2},{6,3},{7,0},{8,13},{9,14},{10,... | collective-permute-start | bytes 49160 | tf_op jit(solution)/shard_map/ppermute | solution.py:342
  26.3 1.9 %collective-permute-start.2 = (bf16[16,4,128]{2,1,0:T(4,128)(2,1)S(1)}, bf16[16,4,128]{2,1,0:T(4,128)(2,1)S(1)}, u32[]{:S(2)}, u32[]{:S(2)}) collective-permute-start(bf16[16,4,128]{2,1,0:T(4,128)(2,1)S(1)} %merge_chips.1.after.refs_0_.finished), channel_id=1, source_target_pairs={{0,6},{1,7},{2,4},{3,5},{4,2},{5,3},{6,0},{7,1},{8,14},{9,15},{10,... | collective-permute-start | bytes 49160 | tf_op jit(solution)/shard_map/ppermute | solution.py:342
  28.2 2.1 %collective-permute-start.1 = (bf16[16,4,128]{2,1,0:T(4,128)(2,1)S(1)}, bf16[16,4,128]{2,1,0:T(4,128)(2,1)S(1)}, u32[]{:S(2)}, u32[]{:S(2)}) collective-permute-start(bf16[16,4,128]{2,1,0:T(4,128)(2,1)S(1)} %merge_chips.1.after.refs_0_.finished), channel_id=1, source_target_pairs={{0,7},{1,4},{2,5},{3,6},{4,3},{5,0},{6,1},{7,2},{8,15},{9,12},{10,... | collective-permute-start | bytes 49160 | tf_op jit(solution)/shard_map/ppermute | solution.py:342
  30.3 3.0 %load_weights.3 = (bf16[208,16384]{1,0:T(8,128)(2,1)S(1)}, bf16[4,16384]{1,0:T(4,128)(2,1)S(1)}, bf16[128,128]{1,0:T(8,128)(2,1)S(1)}) custom-call(bf16[16,4,128]{2,1,0:T(4,128)(2,1)S(1)} %merge_chips.1.after.refs_0_.finished, bf16[208,16384]{1,0:T(8,128)(2,1)} %refs_0_.3, bf16[4,16384]{1,0:T(4,128)(2,1)} %refs_1_.1, bf16[128,128]{1,0:T(8,128)(2,1)} %bitcast.5), custom_call_target="tpu_custom_call" | custom-call | bytes 6979584 | tf_op jit(solution)/shard_map/load_weights/pallas_call | solution.py:257
  33.3 0.0 collective-permute-done.3.refs_3_
  33.3 0.0 collective-permute-done.2.refs_2_
  33.3 0.0 collective-permute-done.1.refs_1_
  33.3 0.1 collective-permute-start.4
  33.4 1.2 %collective-permute-done.4.theirs = bf16[4,16,4,128]{3,2,1,0:T(4,128)(2,1)S(1)} collective-permute-done((bf16[4,16,4,128]{3,2,1,0:T(4,128)(2,1)S(1)}, bf16[4,16,4,128]{3,2,1,0:T(4,128)(2,1)S(1)}, u32[]{:S(2)}, u32[]{:S(2)}) %collective-permute-start.4) | collective-permute-done | bytes 65568 | tf_op jit(solution)/shard_map/ppermute | solution.py:380
  34.7 5.8 %feed_forward.1 = (bf16[128,4,128]{2,1,0:T(4,128)(2,1)S(1)}, f32[4,128]{1,0:T(4,128)S(1)}) custom-call(bf16[4,16,4,128]{3,2,1,0:T(4,128)(2,1)S(1)} %join_heads.1.mine, bf16[4,16,4,128]{3,2,1,0:T(4,128)(2,1)S(1)} %collective-permute-done.4.theirs, bf16[4,16384]{1,0:T(4,128)(2,1)S(1)} %get-tuple-element.12.residual, ...), custom_call_target="tpu_custom_call" | custom-call | tf_op jit(solution)/shard_map/feed_forward/pallas_call | solution.py:381
  40.4 13.8 %all_to_all.11.parts = bf16[128,4,128]{2,1,0:T(4,128)(2,1)S(1)} all-to-all(bf16[128,4,128]{2,1,0:T(4,128)(2,1)S(1)} %get-tuple-element.14), channel_id=1, replica_groups=mesh['chip'=16,'core'=2,'tp'=4] {'chip','core','tp'}, dimensions={0} | all-to-all | bytes 262144 | tf_op jit(solution)/shard_map/all_to_all | solution.py:407
  54.2 0.7 %add_shares.1 = (bf16[4,128]{1,0:T(4,128)(2,1)}, bf16[4,32,128]{2,1,0:T(8,128)(2,1)}) custom-call(bf16[128,4,128]{2,1,0:T(4,128)(2,1)S(1)} %all_to_all.11.parts, f32[4,128]{1,0:T(4,128)S(1)} %get-tuple-element.15.share, bf16[16,4,128]{2,1,0:T(4,128)(2,1)S(1)} %merge_chips.1.after.refs_0_.finished, bf16[4,16,4,128]{3,2,1,0:T(4,128)(2,1)S(1)} %collective-permute-done.4.theirs), custom_call_target="tpu_custom_call" | custom-call | tf_op jit(solution)/shard_map/add_shares/pallas_call | solution.py:331
  (1 shorter events, 0.0 us)
Async XLA Ops:
  4.0 3.0 %collective-permute-start = (f32[16,8,128]{2,1,0:T(8,128)S(1)}, f32[16,8,128]{2,1,0:T(8,128)S(1)}, u32[]{:S(2)}, u32[]{:S(2)}) collective-permute-start(f32[16,8,128]{2,1,0:T(8,128)S(1)} %get-tuple-element.10), channel_id=1, source_target_pairs={{0,4},{4,0},{1,5},{5,1},{2,6},{6,2},{3,7},{7,3},{8,12},{12,8},{9,1... | collective-permute-start | bytes 196616 | tf_op jit(solution)/shard_map/ppermute | solution.py:356
  23.9 9.3 %collective-permute-start.3 = (bf16[16,4,128]{2,1,0:T(4,128)(2,1)S(1)}, bf16[16,4,128]{2,1,0:T(4,128)(2,1)S(1)}, u32[]{:S(2)}, u32[]{:S(2)}) collective-permute-start(bf16[16,4,128]{2,1,0:T(4,128)(2,1)S(1)} %merge_chips.1.after.refs_0_.finished), channel_id=1, source_target_pairs={{0,5},{1,6},{2,7},{3,4},{4,1},{5,2},{6,3},{7,0},{8,13},{9,14},{10,... | collective-permute-start | bytes 49160 | tf_op jit(solution)/shard_map/ppermute | solution.py:342
  26.3 7.0 %collective-permute-start.2 = (bf16[16,4,128]{2,1,0:T(4,128)(2,1)S(1)}, bf16[16,4,128]{2,1,0:T(4,128)(2,1)S(1)}, u32[]{:S(2)}, u32[]{:S(2)}) collective-permute-start(bf16[16,4,128]{2,1,0:T(4,128)(2,1)S(1)} %merge_chips.1.after.refs_0_.finished), channel_id=1, source_target_pairs={{0,6},{1,7},{2,4},{3,5},{4,2},{5,3},{6,0},{7,1},{8,14},{9,15},{10,... | collective-permute-start | bytes 49160 | tf_op jit(solution)/shard_map/ppermute | solution.py:342
  28.2 5.1 %collective-permute-start.1 = (bf16[16,4,128]{2,1,0:T(4,128)(2,1)S(1)}, bf16[16,4,128]{2,1,0:T(4,128)(2,1)S(1)}, u32[]{:S(2)}, u32[]{:S(2)}) collective-permute-start(bf16[16,4,128]{2,1,0:T(4,128)(2,1)S(1)} %merge_chips.1.after.refs_0_.finished), channel_id=1, source_target_pairs={{0,7},{1,4},{2,5},{3,6},{4,3},{5,0},{6,1},{7,2},{8,15},{9,12},{10,... | collective-permute-start | bytes 49160 | tf_op jit(solution)/shard_map/ppermute | solution.py:342
  33.3 1.3 %collective-permute-start.4 = (bf16[4,16,4,128]{3,2,1,0:T(4,128)(2,1)S(1)}, bf16[4,16,4,128]{3,2,1,0:T(4,128)(2,1)S(1)}, u32[]{:S(2)}, u32[]{:S(2)}) collective-permute-start(bf16[4,16,4,128]{3,2,1,0:T(4,128)(2,1)S(1)} %join_heads.1.mine), channel_id=1, source_target_pairs={{0,4},{4,0},{1,5},{5,1},{2,6},{6,2},{3,7},{7,3},{8,12},{12,8},{9,1... | collective-permute-start | bytes 196616 | tf_op jit(solution)/shard_map/ppermute | solution.py:380

commit v7 on v6

--- a/solution.py
+++ b/solution.py
@@ -18,7 +18,7 @@
 CHUNK = 2048
 IN_STEPS = 8
 OUT_STEPS = 4
-UP_HELD = 2
+UP_HELD = 1
 
 
 def kv_index():

time: 55.1 us -> 55.5 us (level)
    pallas_call x1, Pallas kernels: 5.77 us -> 6.47 us  [shards(): pl.pallas_call(feed_kernel, out_shape=[jax.ShapeDtypeStruct((devices, row...]
  transfers between devices with their start and end apart: 5 -> 5, of which waited for: 1 -> 1; matrix products, arithmetic and copies ran while one was open for 0% -> 0% of each run, Pallas kernels for 8% -> 7%
where the time goes in v7:
time: 55.5 us; the launch traced here: 55.3 us
  blocking collectives  29.9 us (54%)
  Pallas kernels  15.4 us (28%)
  starting transfers between devices  7.99 us (14%)
  waiting for transfers between devices  1.25 us (2%)
  between operations  0.73 us (1%)
    all_to_all x1, blocking collectives, shards(): blocks = lax.all_to_all(block, 'chip', 0, 0, tiled=True)  16.1 us
    all_to_all x1, blocking collectives, shards(): sums = lax.all_to_all(mixed, ('chip', 'core', 'tp'), 0, 0, tiled=True)  13.8 us
    pallas_call x1, Pallas kernels, shards(): pl.pallas_call(feed_kernel, out_shape=[jax.ShapeDtypeStruct((devices, row...  6.47 us
    ppermute x3, starting transfers between devices, ring(): lax.ppermute(x, ('core', 'tp'), [(core * tp_size + i, (1 - core) * tp_siz...  6.41 us
    pallas_call x2, Pallas kernels, load(): pl.pallas_call(functools.partial(load_kernel, ranges), out_shape=[pltpu.V...  4.13 us
    pallas_call x1, Pallas kernels, shards(): pl.pallas_call(attention_kernel, out_shape=[block_f32] * 2, in_specs=[HBM...  3.4 us
    ppermute x1, starting transfers between devices, shards(): received = lax.ppermute(send, 'core', swap)  1.5 us
    pallas_call x4, Pallas kernels, call(): pl.pallas_call(kernel, out_shape=out_shape, in_specs=[VMEM] * len(operand...  1.45 us
  transfers between devices with their start and end apart: 5, of which 1 were waited for; matrix products, arithmetic and copies ran while one was open for 0% of the time, Pallas kernels for 7%

profile of v7, /device:TPU:1, one launch (start us, length us, event | category | flops | bytes accessed | tf_op | source)
XLA Modules:
  0.0 55.3 jit_solution(5594072760997055844)
XLA Ops:
  0.6 3.4 %attention_partials.1 = (f32[16,8,128]{2,1,0:T(8,128)S(1)}, f32[16,8,128]{2,1,0:T(8,128)S(1)}) custom-call(s32[4]{0:T(128)} %lengths_h.1, s32[4,64]{1,0:T(4,128)} %table_h.1, bf16[4,32,128]{2,1,0:T(8,128)(2,1)} %query_h.1, bf16[8192,128]{1,0:T(8,128)(2,1)} %bitcast.3, bf16[8192,128]{1,0:T(8,128)(2,1)} %bitcast.4), custom_call_target="tpu_custom_call" | custom-call | tf_op jit(solution)/shard_map/attention_partials/pallas_call | solution.py:313
  4.0 1.5 %collective-permute-start = (f32[16,8,128]{2,1,0:T(8,128)S(1)}, f32[16,8,128]{2,1,0:T(8,128)S(1)}, u32[]{:S(2)}, u32[]{:S(2)}) collective-permute-start(f32[16,8,128]{2,1,0:T(8,128)S(1)} %get-tuple-element.10), channel_id=1, source_target_pairs={{0,4},{4,0},{1,5},{5,1},{2,6},{6,2},{3,7},{7,3},{8,12},{12,8},{9,1... | collective-permute-start | bytes 196616 | tf_op jit(solution)/shard_map/ppermute | solution.py:356
  5.5 1.2 %load_weights.2.loaded.up_first = bf16[208,2048]{1,0:T(8,128)(2,1)S(1)} custom-call(f32[16,8,128]{2,1,0:T(8,128)S(1)} %get-tuple-element.9.after.keep, bf16[208,16384]{1,0:T(8,128)(2,1)} %up_h.1), custom_call_target="tpu_custom_call" | custom-call | bytes 851968 | tf_op jit(solution)/shard_map/load_weights/pallas_call | solution.py:257
  6.7 0.0 collective-permute-done.received
  6.7 0.3 merge_cores.1
  7.0 16.1 %all_to_all.10.parts = bf16[16,17,4,128]{3,2,1,0:T(4,128)(2,1)S(1)} all-to-all(bf16[16,17,4,128]{3,2,1,0:T(4,128)(2,1)S(1)} %merge_cores.1), channel_id=1, replica_groups=mesh['chip'=16,'core'=2,'tp'=4] {'chip'}, dimensions={0} | all-to-all | bytes 557056 | tf_op jit(solution)/shard_map/all_to_all | solution.py:360
  23.1 0.5 merge_chips.1.after.refs_0_.finished
  23.6 2.4 %collective-permute-start.3 = (bf16[16,4,128]{2,1,0:T(4,128)(2,1)S(1)}, bf16[16,4,128]{2,1,0:T(4,128)(2,1)S(1)}, u32[]{:S(2)}, u32[]{:S(2)}) collective-permute-start(bf16[16,4,128]{2,1,0:T(4,128)(2,1)S(1)} %merge_chips.1.after.refs_0_.finished), channel_id=1, source_target_pairs={{0,5},{1,6},{2,7},{3,4},{4,1},{5,2},{6,3},{7,0},{8,13},{9,14},{10,... | collective-permute-start | bytes 49160 | tf_op jit(solution)/shard_map/ppermute | solution.py:342
  26.0 1.8 %collective-permute-start.2 = (bf16[16,4,128]{2,1,0:T(4,128)(2,1)S(1)}, bf16[16,4,128]{2,1,0:T(4,128)(2,1)S(1)}, u32[]{:S(2)}, u32[]{:S(2)}) collective-permute-start(bf16[16,4,128]{2,1,0:T(4,128)(2,1)S(1)} %merge_chips.1.after.refs_0_.finished), channel_id=1, source_target_pairs={{0,6},{1,7},{2,4},{3,5},{4,2},{5,3},{6,0},{7,1},{8,14},{9,15},{10,... | collective-permute-start | bytes 49160 | tf_op jit(solution)/shard_map/ppermute | solution.py:342
  27.9 2.1 %collective-permute-start.1 = (bf16[16,4,128]{2,1,0:T(4,128)(2,1)S(1)}, bf16[16,4,128]{2,1,0:T(4,128)(2,1)S(1)}, u32[]{:S(2)}, u32[]{:S(2)}) collective-permute-start(bf16[16,4,128]{2,1,0:T(4,128)(2,1)S(1)} %merge_chips.1.after.refs_0_.finished), channel_id=1, source_target_pairs={{0,7},{1,4},{2,5},{3,6},{4,3},{5,0},{6,1},{7,2},{8,15},{9,12},{10,... | collective-permute-start | bytes 49160 | tf_op jit(solution)/shard_map/ppermute | solution.py:342
  30.0 3.0 %load_weights.3 = (bf16[208,16384]{1,0:T(8,128)(2,1)S(1)}, bf16[4,16384]{1,0:T(4,128)(2,1)S(1)}, bf16[128,128]{1,0:T(8,128)(2,1)S(1)}) custom-call(bf16[16,4,128]{2,1,0:T(4,128)(2,1)S(1)} %merge_chips.1.after.refs_0_.finished, bf16[208,16384]{1,0:T(8,128)(2,1)} %refs_0_.3, bf16[4,16384]{1,0:T(4,128)(2,1)} %refs_1_.1, bf16[128,128]{1,0:T(8,128)(2,1)} %bitcast.5), custom_call_target="tpu_custom_call" | custom-call | bytes 6979584 | tf_op jit(solution)/shard_map/load_weights/pallas_call | solution.py:257
  33.0 0.0 collective-permute-done.3.refs_3_
  33.0 0.0 collective-permute-done.2.refs_2_
  33.0 0.0 collective-permute-done.1.refs_1_
  33.0 0.1 collective-permute-start.4
  33.1 1.2 %collective-permute-done.4.theirs = bf16[4,16,4,128]{3,2,1,0:T(4,128)(2,1)S(1)} collective-permute-done((bf16[4,16,4,128]{3,2,1,0:T(4,128)(2,1)S(1)}, bf16[4,16,4,128]{3,2,1,0:T(4,128)(2,1)S(1)}, u32[]{:S(2)}, u32[]{:S(2)}) %collective-permute-start.4) | collective-permute-done | bytes 65568 | tf_op jit(solution)/shard_map/ppermute | solution.py:380
  34.4 6.5 %feed_forward.1 = (bf16[128,4,128]{2,1,0:T(4,128)(2,1)S(1)}, f32[4,128]{1,0:T(4,128)S(1)}) custom-call(bf16[4,16,4,128]{3,2,1,0:T(4,128)(2,1)S(1)} %join_heads.1.mine, bf16[4,16,4,128]{3,2,1,0:T(4,128)(2,1)S(1)} %collective-permute-done.4.theirs, bf16[4,16384]{1,0:T(4,128)(2,1)S(1)} %get-tuple-element.12.residual, ...), custom_call_target="tpu_custom_call" | custom-call | tf_op jit(solution)/shard_map/feed_forward/pallas_call | solution.py:381
  40.9 13.8 %all_to_all.11.parts = bf16[128,4,128]{2,1,0:T(4,128)(2,1)S(1)} all-to-all(bf16[128,4,128]{2,1,0:T(4,128)(2,1)S(1)} %get-tuple-element.14), channel_id=1, replica_groups=mesh['chip'=16,'core'=2,'tp'=4] {'chip','core','tp'}, dimensions={0} | all-to-all | bytes 262144 | tf_op jit(solution)/shard_map/all_to_all | solution.py:407
  54.6 0.7 %add_shares.1 = (bf16[4,128]{1,0:T(4,128)(2,1)}, bf16[4,32,128]{2,1,0:T(8,128)(2,1)}) custom-call(bf16[128,4,128]{2,1,0:T(4,128)(2,1)S(1)} %all_to_all.11.parts, f32[4,128]{1,0:T(4,128)S(1)} %get-tuple-element.15.share, bf16[16,4,128]{2,1,0:T(4,128)(2,1)S(1)} %merge_chips.1.after.refs_0_.finished, bf16[4,16,4,128]{3,2,1,0:T(4,128)(2,1)S(1)} %collective-permute-done.4.theirs), custom_call_target="tpu_custom_call" | custom-call | tf_op jit(solution)/shard_map/add_shares/pallas_call | solution.py:331
  (1 shorter events, 0.0 us)
Async XLA Ops:
  4.0 2.7 %collective-permute-start = (f32[16,8,128]{2,1,0:T(8,128)S(1)}, f32[16,8,128]{2,1,0:T(8,128)S(1)}, u32[]{:S(2)}, u32[]{:S(2)}) collective-permute-start(f32[16,8,128]{2,1,0:T(8,128)S(1)} %get-tuple-element.10), channel_id=1, source_target_pairs={{0,4},{4,0},{1,5},{5,1},{2,6},{6,2},{3,7},{7,3},{8,12},{12,8},{9,1... | collective-permute-start | bytes 196616 | tf_op jit(solution)/shard_map/ppermute | solution.py:356
  23.6 9.4 %collective-permute-start.3 = (bf16[16,4,128]{2,1,0:T(4,128)(2,1)S(1)}, bf16[16,4,128]{2,1,0:T(4,128)(2,1)S(1)}, u32[]{:S(2)}, u32[]{:S(2)}) collective-permute-start(bf16[16,4,128]{2,1,0:T(4,128)(2,1)S(1)} %merge_chips.1.after.refs_0_.finished), channel_id=1, source_target_pairs={{0,5},{1,6},{2,7},{3,4},{4,1},{5,2},{6,3},{7,0},{8,13},{9,14},{10,... | collective-permute-start | bytes 49160 | tf_op jit(solution)/shard_map/ppermute | solution.py:342
  26.0 7.0 %collective-permute-start.2 = (bf16[16,4,128]{2,1,0:T(4,128)(2,1)S(1)}, bf16[16,4,128]{2,1,0:T(4,128)(2,1)S(1)}, u32[]{:S(2)}, u32[]{:S(2)}) collective-permute-start(bf16[16,4,128]{2,1,0:T(4,128)(2,1)S(1)} %merge_chips.1.after.refs_0_.finished), channel_id=1, source_target_pairs={{0,6},{1,7},{2,4},{3,5},{4,2},{5,3},{6,0},{7,1},{8,14},{9,15},{10,... | collective-permute-start | bytes 49160 | tf_op jit(solution)/shard_map/ppermute | solution.py:342
  27.9 5.1 %collective-permute-start.1 = (bf16[16,4,128]{2,1,0:T(4,128)(2,1)S(1)}, bf16[16,4,128]{2,1,0:T(4,128)(2,1)S(1)}, u32[]{:S(2)}, u32[]{:S(2)}) collective-permute-start(bf16[16,4,128]{2,1,0:T(4,128)(2,1)S(1)} %merge_chips.1.after.refs_0_.finished), channel_id=1, source_target_pairs={{0,7},{1,4},{2,5},{3,6},{4,3},{5,0},{6,1},{7,2},{8,15},{9,12},{10,... | collective-permute-start | bytes 49160 | tf_op jit(solution)/shard_map/ppermute | solution.py:342
  33.0 1.3 %collective-permute-start.4 = (bf16[4,16,4,128]{3,2,1,0:T(4,128)(2,1)S(1)}, bf16[4,16,4,128]{3,2,1,0:T(4,128)(2,1)S(1)}, u32[]{:S(2)}, u32[]{:S(2)}) collective-permute-start(bf16[4,16,4,128]{3,2,1,0:T(4,128)(2,1)S(1)} %join_heads.1.mine), channel_id=1, source_target_pairs={{0,4},{4,0},{1,5},{5,1},{2,6},{6,2},{3,7},{7,3},{8,12},{12,8},{9,1... | collective-permute-start | bytes 196616 | tf_op jit(solution)/shard_map/ppermute | solution.py:380
